TPU v7x, 32 devices: a whole 2x2x4 slice. The times are simulated.
32 devices in a mesh: row: 4 (over y, x), col: 8 (over z, core).
Axes of the slice: x: 2, y: 2, z: 4, core: 2. Of those that a mesh axis runs over, the one named last changes fastest.
Arguments:
- images: float32 [64, 3, 1024], P(('row', 'col')), may hold values from -16 to 16
- roots: int32 [2, 8], replicated, may hold values from 0 to 3, as said below
Outputs:
- kernel_tiles: float32 [2, 8, 16], P(None, 'row', 'col')
Inputs may be any that keep to these rules, and one draw needn't show every extreme that they name: `roots`: at each tile index every row group appears for exactly 8 / 4 column groups.
All inputs are finite; a program needn't handle non-finite values.
Results may differ from a plain program's by a relative error of at most 0.0001.
Values sent between devices are 32-bit elements; how exact they have to be, the bound alone decides.
No kernel may reach another device: no remote copies, remote signals or barrier semaphores. Data moves between devices by JAX's collectives and lax.ppermute only.
A program may use at most 64 MiB of HBM per device.

v0:
```python
import math

import jax
import jax.numpy as jnp
from jax import lax
from jax.sharding import PartitionSpec as P

WIDTH = 32
CH = 3
DEPTH = 4


weight_var = 2.0
bias_var = 0.1


def from_root(value, axis, source):
    kept = jnp.where(lax.axis_index(axis) == source, value, 0).astype(value.dtype)
    return lax.psum(kept, axis)


def passed_along(block, axis, distance):
    devices = range(lax.axis_size(axis))
    route = [((i - distance) % len(devices), i) for i in devices]
    return lax.ppermute(block, axis, route)


def box_sum(maps):
    positions = lax.broadcasted_iota(jnp.int32, maps.shape, maps.ndim - 1) % WIDTH
    leading = maps.shape[:-1]
    single = jnp.zeros(leading + (1,), jnp.float32)
    band = jnp.zeros(leading + (WIDTH,), jnp.float32)
    from_left = jnp.concatenate([single, maps[..., :-1]], axis=-1)
    from_right = jnp.concatenate([maps[..., 1:], single], axis=-1)
    across = (
        maps
        + jnp.where(positions > 0, from_left, 0.0)
        + jnp.where(positions < WIDTH - 1, from_right, 0.0)
    )
    from_above = jnp.concatenate([band, across[..., :-WIDTH]], axis=-1)
    from_below = jnp.concatenate([across[..., WIDTH:], band], axis=-1)
    return across + from_above + from_below


def relu_map(cross, self_a, self_b):
    scale_ab = jnp.sqrt(self_a * self_b)
    cosine = cross / scale_ab
    return (
        scale_ab
        * (jnp.sqrt(1.0 - cosine * cosine) + (math.pi - jnp.arccos(cosine)) * cosine)
        / (2.0 * math.pi)
    )


def self_maps(pictures):
    energy = jnp.sum(pictures * pictures, axis=1)
    level = weight_var / (9.0 * CH) * box_sum(energy) + bias_var
    stacked = [level]
    for depth_level in range(DEPTH - 1):
        level = weight_var / 9.0 * box_sum(0.5 * level) + bias_var
        stacked.append(level)
    return jnp.stack(stacked, axis=1)


def pair_kernel(row_pictures, col_pictures, row_selfs, col_selfs):
    cross = jnp.einsum("acp,bcp->abp", row_pictures, col_pictures, precision=lax.Precision.HIGHEST)
    level = weight_var / (9.0 * CH) * box_sum(cross) + bias_var
    for depth_level in range(DEPTH - 1):
        mapped = relu_map(level, row_selfs[:, None, depth_level], col_selfs[None, :, depth_level])
        level = weight_var / 9.0 * box_sum(mapped) + bias_var
    final = relu_map(level, row_selfs[:, None, DEPTH - 1], col_selfs[None, :, DEPTH - 1])
    return weight_var * jnp.mean(final, axis=-1) + bias_var


def unpack(payload):
    return (payload, self_maps(payload))


def local(images, roots):
    col_index = lax.axis_index("col")
    column = images
    tiles = []
    for turn_index in range(roots.shape[0]):
        root_group = roots[turn_index, col_index]
        row_load = from_root(images, "row", root_group)
        column = passed_along(column, "col", 1)
        row_pictures, row_selfs = unpack(row_load)
        col_pictures, col_selfs = unpack(column)
        tiles.append(pair_kernel(row_pictures, col_pictures, row_selfs, col_selfs))
    return jnp.stack(tiles)


def solution(mesh):
    in_specs = (P(("row", "col"), None, None), P())
    out_specs = P(None, "row", "col")
    return jax.shard_map(local, mesh=mesh, in_specs=in_specs, out_specs=out_specs, check_vma=False)
```

profile of v0, /device:TPU:0, one launch (start us, length us, event | category | flops | bytes accessed | tf_op | source)
XLA Modules:
  0.0 96.1 jit_solution(13346223398370563292)
XLA Ops:
  0.0 0.5 collective-permute-start
  0.5 0.7 copy-done.29
  1.1 0.7 constant_dynamic-slice_fusion.1
  3.2 18.0 %all-reduce.96 = (f32[2,3,1024]{2,0,1:T(2,128)S(1)}, f32[2,3,1024]{2,1,0:T(4,128)S(1)}) all-reduce(f32[2,3,1024]{2,0,1:T(2,128)S(1)} %broadcast_select_fusion, f32[2,3,1024]{2,1,0:T(4,128)S(1)} %copy_select_fusion), channel_id=1, replica_groups=mesh['row'=4,'col'=8] {'row'}, use_global_device_ids=true, to_apply=%region_4.5 | all-reduce | flops 12288 | bytes 98304 | tf_op jit(solution)/shard_map/psum | solution.py:19
  21.7 1.1 %fusion.97 = (f32[2,1023]{0,1:T(8,128)}, f32[2,1023]{0,1:T(8,128)}) fusion(f32[2,1024]{0,1:T(8,128)S(1)} %copy.90), kind=kLoop, calls=%fused_computation.157 | loop fusion | bytes 32736 | tf_op jit(solution)/shard_map/slice | solution.py:33
  22.8 1.0 %fusion.81 = (f32[2,1023]{0,1:T(8,128)}, f32[2,1023]{0,1:T(8,128)}) fusion(f32[2,1024]{0,1:T(8,128)S(1)} %copy.89), kind=kLoop, calls=%fused_computation.141 | loop fusion | bytes 32736 | tf_op jit(solution)/shard_map/slice | solution.py:33
  23.8 1.3 %copy.70 = f32[2,3,1024]{1,0,2:T(2,128)} copy(f32[2,3,1024]{2,1,0:T(4,128)S(1)} %get-tuple-element.6) | data formatting | bytes 49152 | tf_op jit(solution)/shard_map/psum | solution.py:19
  25.1 0.5 copy.86
  25.9 1.3 %copy.71 = f32[2,3,1024]{1,0,2:T(2,128)} copy(f32[2,3,1024]{2,0,1:T(2,128)S(1)} %collective-permute-done) | data formatting | bytes 49152 | tf_op jit(solution)/shard_map/ppermute | solution.py:25
  27.2 9.5 %fusion.116 = f32[1024,2,2]{2,1,0:T(2,128)} fusion(f32[2,3,1024]{1,0,2:T(2,128)} %copy.70, f32[2,3,1024]{1,0,2:T(2,128)} %copy.71), kind=kOutput, calls=%fused_computation.176 | convolution fusion | flops 147456 | bytes 65536 | tf_op jit(solution)/shard_map/acp,bcp->abp/dot_general | solution.py:66
  36.7 1.4 %copy.72 = f32[1024,2,2]{0,2,1:T(2,128)S(1)} copy(f32[1024,2,2]{2,1,0:T(2,128)} %fusion.116) | data formatting | bytes 32768 | tf_op jit(solution)/shard_map/acp,bcp->abp/dot_general | solution.py:66
  38.2 1.1 %fusion.83 = (f32[2,1023]{0,1:T(8,128)}, f32[2,1023]{0,1:T(8,128)}) fusion(f32[2,1024]{0,1:T(8,128)S(1)} %copy.61), kind=kLoop, calls=%fused_computation.143 | loop fusion | bytes 32736 | tf_op jit(solution)/shard_map/slice | solution.py:33
  39.4 0.2 collective-permute-start.1
  39.7 5.0 %collective-permute-done.1 = f32[2,3,1024]{2,0,1:T(2,128)S(1)} collective-permute-done((f32[2,3,1024]{2,0,1:T(2,128)S(1)}, f32[2,3,1024]{2,0,1:T(2,128)S(1)}, u32[]{:S(2)}, u32[]{:S(2)}) %collective-permute-start.1) | collective-permute-done | bytes 24608 | tf_op jit(solution)/shard_map/ppermute | solution.py:25
  44.9 1.3 %copy.87 = f32[2,3,1024]{1,0,2:T(2,128)} copy(f32[2,3,1024]{2,0,1:T(2,128)S(1)} %collective-permute-done.1) | data formatting | bytes 49152 | tf_op jit(solution)/shard_map/ppermute | solution.py:25
  46.2 9.0 %fusion.117 = f32[1024,2,2]{2,1,0:T(2,128)} fusion(f32[2,3,1024]{1,0,2:T(2,128)S(1)} %copy.86, f32[2,3,1024]{1,0,2:T(2,128)} %copy.87), kind=kOutput, calls=%fused_computation.177 | convolution fusion | flops 147456 | bytes 65536 | tf_op jit(solution)/shard_map/acp,bcp->abp/dot_general | solution.py:66
  55.2 1.4 %copy.88 = f32[1024,2,2]{0,2,1:T(2,128)S(1)} copy(f32[1024,2,2]{2,1,0:T(2,128)} %fusion.117) | data formatting | bytes 32768 | tf_op jit(solution)/shard_map/acp,bcp->abp/dot_general | solution.py:66
  56.8 0.9 copy-done.18
  58.2 2.4 %fusion.32 = (f32[2,1024]{0,1:T(8,128)S(1)}, f32[2,1024]{0,1:T(8,128)S(1)}, f32[2,1024]{0,1:T(8,128)S(1)}, f32[2,1024]{0,1:T(8,128)S(1)}) fusion(f32[2,1024]{0,1:T(8,128)S(1)} %copy.89, f32[2,1023]{0,1:T(8,128)S(1)} %copy-done.21, f32[2,1023]{0,1:T(8,128)S(1)} %copy-done.20, s32[1024]{0:T(1024)S(1)} %iota_and_fusion, s32[1024]{0:T(1024)S(1)} %fusion.64, ...), kind=kLoop, calls=%fused_computation.34 | loop fusion | flops 38912 | bytes 140224 | tf_op jit(solution)/shard_map/add | solution.py:36
  60.6 1.1 %fusion.80 = (f32[2,992]{0,1:T(8,128)}, f32[2,992]{0,1:T(8,128)}) fusion(f32[2,1024]{0,1:T(8,128)S(1)} %get-tuple-element.141), kind=kLoop, calls=%fused_computation.140 | loop fusion | bytes 31744 | tf_op jit(solution)/shard_map/slice | solution.py:40
  61.8 0.3 broadcast_multiply_fusion.2
  62.4 0.4 copy-done.2
  62.9 1.0 %fusion.95 = (f32[2,1023]{0,1:T(8,128)}, f32[2,1023]{0,1:T(8,128)}) fusion(f32[2,1024]{0,1:T(8,128)S(1)} %get-tuple-element.29), kind=kLoop, calls=%fused_computation.155 | loop fusion | bytes 32736 | tf_op jit(solution)/shard_map/slice | solution.py:33
  64.0 1.0 %copy-done.26 = f32[2,992]{0,1:T(8,128)S(1)} copy-done((f32[2,992]{0,1:T(8,128)S(1)}, f32[2,992]{0,1:T(8,128)}, u32[]{:S(2)}) %copy-start.26) | copy-done | bytes 7960
  65.1 1.3 %broadcast_multiply_fusion.8 = (f32[2,1024]{0,1:T(8,128)}, f32[2,1024]{0,1:T(8,128)S(1)}, f32[2,1024]{0,1:T(8,128)}, f32[2,1024]{0,1:T(8,128)S(1)}) fusion(f32[2,992]{0,1:T(8,128)S(1)} %get-tuple-element.60, f32[2,1024]{0,1:T(8,128)S(1)} %get-tuple-element.144, f32[2,992]{0,1:T(8,128)S(1)} %get-tuple-element.59, f32[2,992]{0,1:T(8,128)S(1)} %copy-done.27, ...), kind=kLoop, calls=%fused_computation.90 | loop fusion | flops 20480 | bytes 80896 | tf_op jit(solution)/shard_map/mul | solution.py:60
  66.7 0.4 copy-done.4
  67.4 0.3 multiply_multiply_fusion.5
  68.0 1.0 copy-done.9
  69.1 0.8 copy-done.25
  70.6 1.6 %fusion.33 = (f32[2,1024]{0,1:T(8,128)S(1)}, f32[2,1024]{0,1:T(8,128)S(1)}, f32[2,1024]{0,1:T(8,128)S(1)}, f32[2,1024]{0,1:T(8,128)S(1)}) fusion(f32[2,1023]{0,1:T(8,128)S(1)} %get-tuple-element.50, f32[2,1023]{0,1:T(8,128)S(1)} %get-tuple-element.49, s32[1024]{0:T(1024)S(1)} %iota_and_fusion, s32[1024]{0:T(1024)S(1)} %fusion.64, ...), kind=kLoop, calls=%fused_computation.35 | loop fusion | flops 47104 | bytes 140224 | tf_op jit(solution)/shard_map/add | solution.py:36
  72.6 1.1 %fusion.73 = (f32[2,1023]{0,1:T(8,128)}, f32[2,1023]{0,1:T(8,128)}) fusion(f32[2,1024]{0,1:T(8,128)S(1)} %get-tuple-element.11), kind=kLoop, calls=%fused_computation.133 | loop fusion | bytes 32736 | tf_op jit(solution)/shard_map/slice | solution.py:33
  74.1 1.0 %fusion.91 = (f32[2,1023]{0,1:T(8,128)}, f32[2,1023]{0,1:T(8,128)}) fusion(f32[2,1024]{0,1:T(8,128)S(1)} %get-tuple-element.25), kind=kLoop, calls=%fused_computation.151 | loop fusion | bytes 32736 | tf_op jit(solution)/shard_map/slice | solution.py:33
  75.5 1.1 %fusion.89 = (f32[2,1023]{0,1:T(8,128)}, f32[2,1023]{0,1:T(8,128)}) fusion(f32[2,1024]{0,1:T(8,128)S(1)} %get-tuple-element.23), kind=kLoop, calls=%fused_computation.149 | loop fusion | bytes 32736 | tf_op jit(solution)/shard_map/slice | solution.py:33
  77.0 0.3 multiply_multiply_fusion.4
  77.7 0.9 copy-done.16
  79.1 2.7 %fusion.34 = (f32[2,1024]{0,1:T(8,128)S(1)}, f32[2,1024]{0,1:T(8,128)S(1)}, f32[2,1024]{0,1:T(8,128)S(1)}, f32[2,1024]{0,1:T(8,128)S(1)}) fusion(f32[2,1023]{0,1:T(8,128)S(1)} %copy-done.17, f32[2,1023]{0,1:T(8,128)S(1)} %copy-done.16, s32[1024]{0:T(1024)S(1)} %iota_and_fusion, s32[1024]{0:T(1024)S(1)} %fusion.64, pred[1024]{0:T(1024)(128)(4,1)S(1)} %fusion.67, ...), kind=kLoop, calls=%fused_computation.36 | loop fusion | flops 47104 | bytes 140224 | tf_op jit(solution)/shard_map/add | solution.py:36
  82.2 1.1 %fusion.69 = (f32[2,1023]{0,1:T(8,128)}, f32[2,1023]{0,1:T(8,128)}) fusion(f32[2,1024]{0,1:T(8,128)S(1)} %get-tuple-element.7), kind=kLoop, calls=%fused_computation.129 | loop fusion | bytes 32736 | tf_op jit(solution)/shard_map/slice | solution.py:33
  83.7 1.0 %fusion.87 = (f32[2,1023]{0,1:T(8,128)}, f32[2,1023]{0,1:T(8,128)}) fusion(f32[2,1024]{0,1:T(8,128)S(1)} %get-tuple-element.21), kind=kLoop, calls=%fused_computation.147 | loop fusion | bytes 32736 | tf_op jit(solution)/shard_map/slice | solution.py:33
  85.1 1.1 %fusion.85 = (f32[2,1023]{0,1:T(8,128)}, f32[2,1023]{0,1:T(8,128)}) fusion(f32[2,1024]{0,1:T(8,128)S(1)} %get-tuple-element.19), kind=kLoop, calls=%fused_computation.145 | loop fusion | bytes 32736 | tf_op jit(solution)/shard_map/slice | solution.py:33
  86.6 0.3 multiply_multiply_fusion.3
  87.2 0.3 multiply_multiply_fusion.2
  87.8 0.3 multiply_multiply_fusion.1
  88.3 0.3 multiply_multiply_fusion
  89.0 0.9 copy-done.1
  90.4 2.8 %fusion.35 = (f32[2,1024]{0,1:T(8,128)S(1)}, f32[2,1024]{0,1:T(8,128)S(1)}, f32[2,1024]{0,1:T(8,128)S(1)}, f32[2,1024]{0,1:T(8,128)S(1)}) fusion(f32[2,1023]{0,1:T(8,128)S(1)} %copy-done.12, f32[2,1023]{0,1:T(8,128)S(1)} %copy-done.11, s32[1024]{0:T(1024)S(1)} %iota_and_fusion, s32[1024]{0:T(1024)S(1)} %fusion.64, pred[1024]{0:T(1024)(128)(4,1)S(1)} %fusion.67, ...), kind=kLoop, calls=%fused_computation.37 | loop fusion | flops 47104 | bytes 140224 | tf_op jit(solution)/shard_map/add | solution.py:36
  94.4 0.3 multiply_reduce_fusion.4
  95.2 0.3 multiply_reduce_fusion.5
  95.5 0.6 pad_maximum_fusion
  (139 shorter events, 11.5 us)
Async XLA Ops:
  0.0 3.1 %copy-start.28 = (f32[2,3,1024]{2,0,1:T(2,128)S(1)}, f32[2,3,1024]{2,0,1:T(2,128)}, u32[]{:S(2)}) copy-start(f32[2,3,1024]{2,0,1:T(2,128)} %param.2) | copy-start | bytes 73732
  0.0 25.6 %collective-permute-start = (f32[2,3,1024]{2,0,1:T(2,128)}, f32[2,3,1024]{2,0,1:T(2,128)S(1)}, u32[]{:S(2)}, u32[]{:S(2)}) collective-permute-start(f32[2,3,1024]{2,0,1:T(2,128)} %param.2), channel_id=1, source_target_pairs={{7,0},{0,1},{1,2},{2,3},{3,4},{4,5},{5,6},{6,7},{15,8},{8,9},{9,10... | collective-permute-start | bytes 73736 | tf_op jit(solution)/shard_map/ppermute | solution.py:25
  0.5 0.7 copy-start.29
  39.4 5.3 %collective-permute-start.1 = (f32[2,3,1024]{2,0,1:T(2,128)S(1)}, f32[2,3,1024]{2,0,1:T(2,128)S(1)}, u32[]{:S(2)}, u32[]{:S(2)}) collective-permute-start(f32[2,3,1024]{2,0,1:T(2,128)S(1)} %collective-permute-done), channel_id=1, source_target_pairs={{7,0},{0,1},{1,2},{2,3},{3,4},{4,5},{5,6},{6,7},{15,8},{8,9},{9,10... | collective-permute-start | bytes 73736 | tf_op jit(solution)/shard_map/ppermute | solution.py:25
  56.7 1.1 %copy-start.18 = (f32[2,1023]{0,1:T(8,128)S(1)}, f32[2,1023]{0,1:T(8,128)}, u32[]{:S(2)}) copy-start(f32[2,1023]{0,1:T(8,128)} %get-tuple-element.89) | copy-start | bytes 24556
  56.7 1.2 %copy-start.19 = (f32[2,1023]{0,1:T(8,128)S(1)}, f32[2,1023]{0,1:T(8,128)}, u32[]{:S(2)}) copy-start(f32[2,1023]{0,1:T(8,128)} %get-tuple-element.90) | copy-start | bytes 24556
  56.7 1.4 %copy-start.20 = (f32[2,1023]{0,1:T(8,128)S(1)}, f32[2,1023]{0,1:T(8,128)}, u32[]{:S(2)}) copy-start(f32[2,1023]{0,1:T(8,128)} %get-tuple-element.57) | copy-start | bytes 24556
  56.7 1.5 %copy-start.21 = (f32[2,1023]{0,1:T(8,128)S(1)}, f32[2,1023]{0,1:T(8,128)}, u32[]{:S(2)}) copy-start(f32[2,1023]{0,1:T(8,128)} %get-tuple-element.58) | copy-start | bytes 24556
  62.1 0.8 copy-start.2
  63.9 1.0 %copy-start.26 = (f32[2,992]{0,1:T(8,128)S(1)}, f32[2,992]{0,1:T(8,128)}, u32[]{:S(2)}) copy-start(f32[2,992]{0,1:T(8,128)} %get-tuple-element.55) | copy-start | bytes 23812
  63.9 1.2 %copy-start.27 = (f32[2,992]{0,1:T(8,128)S(1)}, f32[2,992]{0,1:T(8,128)}, u32[]{:S(2)}) copy-start(f32[2,992]{0,1:T(8,128)} %get-tuple-element.56) | copy-start | bytes 23812
  66.4 0.8 copy-start.4
  66.4 1.0 %copy-start.6 = (f32[2,1024]{0,1:T(8,128)}, f32[2,1024]{0,1:T(8,128)S(1)}, u32[]{:S(2)}) copy-start(f32[2,1024]{0,1:T(8,128)S(1)} %get-tuple-element.150) | copy-start | bytes 24580
  66.5 1.3 %copy-start.10 = (f32[2,1024]{0,1:T(8,128)S(1)}, f32[2,1024]{0,1:T(8,128)}, u32[]{:S(2)}) copy-start(f32[2,1024]{0,1:T(8,128)} %get-tuple-element.17) | copy-start | bytes 24580
  67.9 1.0 %copy-start.9 = (f32[2,1024]{0,1:T(8,128)S(1)}, f32[2,1024]{0,1:T(8,128)}, u32[]{:S(2)}) copy-start(f32[2,1024]{0,1:T(8,128)} %get-tuple-element.149) | copy-start | bytes 24580
  68.9 1.0 %copy-start.25 = (f32[2,1023]{0,1:T(8,128)S(1)}, f32[2,1023]{0,1:T(8,128)}, u32[]{:S(2)}) copy-start(f32[2,1023]{0,1:T(8,128)} %get-tuple-element.86) | copy-start | bytes 24556
  69.0 1.1 %copy-start.3 = (f32[2,1024]{0,1:T(8,128)S(1)}, f32[2,1024]{0,1:T(8,128)}, u32[]{:S(2)}) copy-start(f32[2,1024]{0,1:T(8,128)} %copy-done.2) | copy-start | bytes 24580
  69.0 1.3 %copy-start.5 = (f32[2,1024]{0,1:T(8,128)S(1)}, f32[2,1024]{0,1:T(8,128)}, u32[]{:S(2)}) copy-start(f32[2,1024]{0,1:T(8,128)} %copy-done.4) | copy-start | bytes 24580
  69.0 1.4 %copy-start.7 = (f32[2,1024]{0,1:T(8,128)S(1)}, f32[2,1024]{0,1:T(8,128)}, u32[]{:S(2)}) copy-start(f32[2,1024]{0,1:T(8,128)} %copy-done.6) | copy-start | bytes 24580
  69.0 1.6 %copy-start.24 = (f32[2,1023]{0,1:T(8,128)S(1)}, f32[2,1023]{0,1:T(8,128)}, u32[]{:S(2)}) copy-start(f32[2,1023]{0,1:T(8,128)} %get-tuple-element.85) | copy-start | bytes 24556
  76.8 0.8 copy-start.8
  77.5 1.1 %copy-start.16 = (f32[2,1023]{0,1:T(8,128)S(1)}, f32[2,1023]{0,1:T(8,128)}, u32[]{:S(2)}) copy-start(f32[2,1023]{0,1:T(8,128)} %get-tuple-element.41) | copy-start | bytes 24556
  77.5 1.2 %copy-start.17 = (f32[2,1023]{0,1:T(8,128)S(1)}, f32[2,1023]{0,1:T(8,128)}, u32[]{:S(2)}) copy-start(f32[2,1023]{0,1:T(8,128)} %get-tuple-element.42) | copy-start | bytes 24556
  77.6 1.4 %copy-start.22 = (f32[2,1023]{0,1:T(8,128)S(1)}, f32[2,1023]{0,1:T(8,128)}, u32[]{:S(2)}) copy-start(f32[2,1023]{0,1:T(8,128)} %get-tuple-element.77) | copy-start | bytes 24556
  77.6 1.5 %copy-start.23 = (f32[2,1023]{0,1:T(8,128)S(1)}, f32[2,1023]{0,1:T(8,128)}, u32[]{:S(2)}) copy-start(f32[2,1023]{0,1:T(8,128)} %get-tuple-element.78) | copy-start | bytes 24556
  86.4 1.1 %copy-start = (f32[2,1024]{0,1:T(8,128)}, f32[2,1024]{0,1:T(8,128)S(1)}, u32[]{:S(2)}) copy-start(f32[2,1024]{0,1:T(8,128)S(1)} %get-tuple-element.10) | copy-start | bytes 24580
  86.9 2.0 %copy-start.15 = (f32[2,1023]{0,1:T(8,128)S(1)}, f32[2,1023]{0,1:T(8,128)}, u32[]{:S(2)}) copy-start(f32[2,1023]{0,1:T(8,128)} %get-tuple-element.65) | copy-start | bytes 24556
  87.7 1.3 %copy-start.14 = (f32[2,1023]{0,1:T(8,128)S(1)}, f32[2,1023]{0,1:T(8,128)}, u32[]{:S(2)}) copy-start(f32[2,1023]{0,1:T(8,128)} %get-tuple-element.70) | copy-start | bytes 24556
  88.9 1.1 %copy-start.1 = (f32[2,1024]{0,1:T(8,128)S(1)}, f32[2,1024]{0,1:T(8,128)}, u32[]{:S(2)}) copy-start(f32[2,1024]{0,1:T(8,128)} %copy-done) | copy-start | bytes 24580
  88.9 1.2 %copy-start.11 = (f32[2,1023]{0,1:T(8,128)S(1)}, f32[2,1023]{0,1:T(8,128)}, u32[]{:S(2)}) copy-start(f32[2,1023]{0,1:T(8,128)} %get-tuple-element.33) | copy-start | bytes 24556
  88.9 1.4 %copy-start.12 = (f32[2,1023]{0,1:T(8,128)S(1)}, f32[2,1023]{0,1:T(8,128)}, u32[]{:S(2)}) copy-start(f32[2,1023]{0,1:T(8,128)} %get-tuple-element.34) | copy-start | bytes 24556
  88.9 1.5 %copy-start.13 = (f32[2,1023]{0,1:T(8,128)S(1)}, f32[2,1023]{0,1:T(8,128)}, u32[]{:S(2)}) copy-start(f32[2,1023]{0,1:T(8,128)} %get-tuple-element.69) | copy-start | bytes 24556
where the time goes:
time: 96.7 us; the launch traced here: 96.1 us
  local copies, waits for them, and re-layouts  35.6 us (37%)
  matrix products  18.5 us (19%)
  blocking collectives  18 us (19%)
  other arithmetic  16.4 us (17%)
  waiting for transfers between devices  4.96 us (5%)
  between operations  1.97 us (2%)
    dot_general x2, matrix products, pair_kernel(): jnp.einsum('acp,bcp->abp', row_pictures, col_pictures, precision=lax.Prec...  18.5 us
    psum x1, blocking collectives, from_root(): return lax.psum(kept, axis)  18 us
    slice x24, local copies, waits for them, and re-layouts, box_sum(): from_left = jnp.concatenate([single, maps[..., :-1]], axis=-1)  11.6 us
    add x11, other arithmetic, box_sum(): maps + jnp.where(positions > 0, from_left, 0.0)  10.1 us
    unnamed x62, local copies, waits for them, and re-layouts  10 us
    ppermute x2, waiting for transfers between devices, passed_along(): return lax.ppermute(block, axis, route)  4.96 us
    dot_general x2, local copies, waits for them, and re-layouts, pair_kernel(): jnp.einsum('acp,bcp->abp', row_pictures, col_pictures, precision=lax.Prec...  2.84 us
    slice x24, local copies, waits for them, and re-layouts, box_sum(): from_above = jnp.concatenate([band, across[..., :-WIDTH]], axis=-1)  2.71 us
  transfers between devices with their start and end apart: 2, of which 1 were waited for; matrix products, arithmetic and copies ran while one was open for 5% of the time, Pallas kernels for 0%

commit v1 on v0

v1 whole, which is shorter than its diff:
```python
import math

import jax
import jax.numpy as jnp
import numpy as np
from jax import lax
from jax.experimental import pallas as pl
from jax.experimental.pallas import tpu as pltpu
from jax.sharding import PartitionSpec as P

WIDTH = 32
LANES = 128
DEPTH = 4

weight_var = 2.0
bias_var = 0.1


def remainder_coefficients(degree=6, nodes=64):
    u = 0.5 + 0.5 * np.cos(np.pi * (np.arange(nodes) + 0.5) / nodes)
    angle = 2.0 * np.arcsin(np.sqrt(0.5 * u))
    series = sum(
        (-1) ** n * 2.0 * n / math.factorial(2 * n + 1) * angle ** (2 * n + 1) * -1.0
        for n in range(1, 8)
    )
    exact = np.sin(angle) - angle * np.cos(angle)
    q = np.where(angle < 0.5, series, exact) / u**1.5
    fit = np.polynomial.chebyshev.Chebyshev.fit(u, q, degree, domain=[0.0, 1.0])
    return fit.convert(kind=np.polynomial.Polynomial).coef


COEFS = [float(v) / (2.0 * math.pi) for v in remainder_coefficients()]


def kernel(powers, n_row, roots_ref, *refs):
    n_tiles = roots_ref.shape[0]
    row_refs, col_refs, out_ref = refs[:n_row], refs[n_row:-1], refs[-1]
    row_index, col_index = lax.axis_index("row"), lax.axis_index("col")
    block = row_refs[0].shape[0] // 24
    rows = 8 * block
    sub = lax.broadcasted_iota(jnp.int32, (rows, LANES), 0)
    lane = lax.broadcasted_iota(jnp.int32, (rows, LANES), 1)
    not_left = (lane % WIDTH) != 0
    not_right = (lane % WIDTH) != WIDTH - 1
    first_band = lane < WIDTH
    last_band = lane >= LANES - WIDTH
    above_inside = jnp.logical_and(first_band, sub >= block)
    below_inside = jnp.logical_and(last_band, sub < rows - block)
    even = (sub % 2) == 0

    def box(m):
        left = jnp.where(not_left, pltpu.roll(m, 1, 1), 0.0)
        right = jnp.where(not_right, pltpu.roll(m, LANES - 1, 1), 0.0)
        across = m + left + right
        down = pltpu.roll(across, WIDTH, 1)
        up = pltpu.roll(across, LANES - WIDTH, 1)
        down_far = jnp.where(above_inside, pltpu.roll(down, block, 0), 0.0)
        up_far = jnp.where(below_inside, pltpu.roll(up, rows - block, 0), 0.0)
        return across + jnp.where(first_band, down_far, down) + jnp.where(last_band, up_far, up)

    def swapped(m):
        return jnp.where(even, pltpu.roll(m, rows - 1, 0), pltpu.roll(m, 1, 0))

    def channels(value):
        return [value[c * rows:(c + 1) * rows] for c in range(3)]

    def self_maps(value):
        energy = sum(v * v for v in channels(value))
        level = weight_var / 27.0 * box(energy) + bias_var
        levels = [level]
        for _ in range(DEPTH - 1):
            level = box(weight_var / 18.0 * level) + bias_var
            levels.append(level)
        inverse = [lax.rsqrt(v) for v in levels]
        return [v * r for v, r in zip(levels, inverse)], inverse

    def relu_map(k, scale, inverse):
        c = k * inverse
        u = jnp.maximum(1.0 - jnp.abs(c), 0.0)
        poly = jnp.full_like(u, COEFS[-1])
        for coef in COEFS[-2::-1]:
            poly = poly * u + coef
        return 0.5 * jnp.maximum(k, 0.0) + scale * (u * jnp.sqrt(u)) * poly

    sums = []
    for s in range(n_tiles):
        root = roots_ref[s, col_index]
        source = root ^ row_index if powers else lax.rem(row_index - root + n_row, n_row)
        row_value = row_refs[0][...]
        for k in range(1, n_row):
            row_value = jnp.where(source == k, row_refs[k][...], row_value)
        col_value = col_refs[s][...]
        row_std, row_inv = self_maps(row_value)
        col_std, col_inv = self_maps(col_value)
        for d in range(2):
            if d:
                col_std = [swapped(v) for v in col_std]
                col_inv = [swapped(v) for v in col_inv]
            turn = swapped if d else lambda v: v
            cross = sum(a * turn(b) for a, b in zip(channels(row_value), channels(col_value)))
            level = weight_var / 27.0 * box(cross) + bias_var
            for l in range(DEPTH):
                mapped = relu_map(level, row_std[l] * col_std[l], row_inv[l] * col_inv[l])
                if l < DEPTH - 1:
                    level = weight_var / 9.0 * box(mapped) + bias_var
            total = mapped[:8] + mapped[8:]
            total = total + pltpu.roll(total, 4, 0)
            sums.append(total + pltpu.roll(total, 2, 0))
    sub8 = sub[:8]
    packed = sums[0]
    for q in range(8):
        s, a, b = (q // 2) % 2, q % 2, q // 4
        packed = jnp.where(sub8 == q, sums[2 * s + (a ^ b)], packed)
    mean = jnp.sum(packed, axis=1, keepdims=True) * (1.0 / 1024.0)
    value = jnp.broadcast_to(weight_var * mean + bias_var, (8, LANES))
    result = jnp.where(lane[:8] == 0, value, pltpu.roll(value, 4, 0))
    for s in range(n_tiles):
        out_ref[s] = result[2 * s:2 * s + 2, 0:2]


def local(images, roots):
    n_row, n_col = lax.axis_size("row"), lax.axis_size("col")
    n_tiles = roots.shape[0]
    block, ch, pix = images.shape
    tiles = pix // LANES
    packed = images.reshape(block, ch, tiles, LANES).transpose(1, 2, 0, 3).reshape(ch * tiles * block, LANES)
    powers = n_row & (n_row - 1) == 0
    row_blocks = [packed]
    for k in range(1, n_row):
        if powers:
            route = [(i, i ^ k) for i in range(n_row)]
        else:
            route = [(i, (i + k) % n_row) for i in range(n_row)]
        row_blocks.append(lax.ppermute(packed, "row", route))
    col_blocks = [
        lax.ppermute(packed, "col", [(i, (i + s + 1) % n_col) for i in range(n_col)])
        for s in range(n_tiles)
    ]
    vmem = pl.BlockSpec(memory_space=pltpu.VMEM)
    return pl.pallas_call(
        lambda *refs: kernel(powers, n_row, *refs),
        out_shape=jax.ShapeDtypeStruct((n_tiles, block, block), jnp.float32),
        in_specs=[pl.BlockSpec(memory_space=pltpu.SMEM)] + [vmem] * (n_row + n_tiles),
        out_specs=vmem,
        name="tiles",
    )(roots, *row_blocks, *col_blocks)


def solution(mesh):
    in_specs = (P(("row", "col"), None, None), P())
    out_specs = P(None, "row", "col")
    return jax.shard_map(local, mesh=mesh, in_specs=in_specs, out_specs=out_specs, check_vma=False)
```

time: 96.7 us -> 13.3 us (0.14)
  local copies, waits for them, and re-layouts: 35.6 us -> 0.61 us
  matrix products: 18.5 us -> 0 us
  blocking collectives: 18 us -> 0 us
  other arithmetic: 16.4 us -> 0 us
  starting transfers between devices: 0.69 us -> 6.51 us
  Pallas kernels: 0 us -> 2.27 us
  between operations: 1.97 us -> 0.03 us
  waiting for transfers between devices: 4.96 us -> 3.6 us
    dot_general x2 -> x0, matrix products: 18.5 us -> none  [pair_kernel(): jnp.einsum('acp,bcp->abp', row_pictures, col_pictures, precision=lax.Prec...]
    psum x1 -> x0, blocking collectives: 18 us -> none  [from_root(): return lax.psum(kept, axis)]
    slice x48 -> x0, local copies, waits for them, and re-layouts: 14.3 us -> none  [the longest x24 11.6 us: box_sum(): from_left = jnp.concatenate([single, maps[..., :-1]], axis=-1)]
    add x18 -> x0, other arithmetic: 10.7 us -> none  [the longest x11 10.1 us: box_sum(): maps + jnp.where(positions > 0, from_left, 0.0)]
    unnamed x62 -> x10, local copies, waits for them, and re-layouts: 10 us -> 0.61 us
    ppermute x2 -> x5, starting transfers between devices: 0.69 us -> 6.51 us  [the longest x3 3.49 us: local(): row_blocks.append(lax.ppermute(packed, 'row', route))]
    add x16 -> x0, local copies, waits for them, and re-layouts: 2.96 us -> none  [the longest x12 2.2 us: self_maps(): level = weight_var / 9.0 * box_sum(0.5 * level) + bias_var]
    dot_general x2 -> x0, local copies, waits for them, and re-layouts: 2.84 us -> none  [pair_kernel(): jnp.einsum('acp,bcp->abp', row_pictures, col_pictures, precision=lax.Prec...]
  transfers between devices with their start and end apart: 2 -> 5, of which waited for: 1 -> 4; matrix products, arithmetic and copies ran while one was open for 5% -> 0% of each run, Pallas kernels for 0% -> 0%
where the time goes in v1:
time: 13.3 us; the launch traced here: 13 us
  starting transfers between devices  6.51 us (49%)
  waiting for transfers between devices  3.6 us (27%)
  Pallas kernels  2.27 us (17%)
  local copies, waits for them, and re-layouts  0.61 us (5%)
    ppermute x3, starting transfers between devices, local(): row_blocks.append(lax.ppermute(packed, 'row', route))  3.49 us
    ppermute x2, starting transfers between devices, local(): lax.ppermute(packed, 'col', [(i, (i + s + 1) % n_col) for i in range(n_co...  3.03 us
    pallas_call x1, Pallas kernels, local(): pl.pallas_call(lambda *refs: kernel(powers, n_row, *refs), out_shape=jax....  2.27 us
    ppermute x3, waiting for transfers between devices, local(): row_blocks.append(lax.ppermute(packed, 'row', route))  1.83 us
    ppermute x2, waiting for transfers between devices, local(): lax.ppermute(packed, 'col', [(i, (i + s + 1) % n_col) for i in range(n_co...  1.76 us
    unnamed x10, local copies, waits for them, and re-layouts  0.61 us
  transfers between devices with their start and end apart: 5, of which 4 were waited for; matrix products, arithmetic and copies ran while one was open for 0% of the time, Pallas kernels for 0%

profile of v1, /device:TPU:0, one launch (start us, length us, event | category | flops | bytes accessed | tf_op | source)
XLA Modules:
  0.0 13.0 jit_solution(17574906104604529926)
XLA Ops:
  0.0 3.0 %collective-permute-start.4 = (f32[48,128]{1,0:T(8,128)}, f32[48,128]{1,0:T(8,128)S(1)}, u32[]{:S(2)}, u32[]{:S(2)}) collective-permute-start(f32[48,128]{1,0:T(8,128)} %bitcast.5), channel_id=1, source_target_pairs={{0,2},{1,3},{2,4},{3,5},{4,6},{5,7},{6,0},{7,1},{8,10},{9,11},{10,... | collective-permute-start | bytes 73736 | tf_op jit(solution)/shard_map/ppermute | solution.py:136
  3.0 0.0 collective-permute-start.3
  3.0 2.4 %collective-permute-start.2 = (f32[48,128]{1,0:T(8,128)}, f32[48,128]{1,0:T(8,128)S(1)}, u32[]{:S(2)}, u32[]{:S(2)}) collective-permute-start(f32[48,128]{1,0:T(8,128)} %bitcast.7), channel_id=1, source_target_pairs={{0,24},{8,16},{16,8},{24,0},{1,25},{9,17},{17,9},{25,1},{2,26},{10... | collective-permute-start | bytes 73736 | tf_op jit(solution)/shard_map/ppermute | solution.py:134
  5.5 0.5 %collective-permute-start.1 = (f32[48,128]{1,0:T(8,128)}, f32[48,128]{1,0:T(8,128)S(1)}, u32[]{:S(2)}, u32[]{:S(2)}) collective-permute-start(f32[48,128]{1,0:T(8,128)} %bitcast.8), channel_id=1, source_target_pairs={{0,16},{8,24},{16,0},{24,8},{1,17},{9,25},{17,1},{25,9},{2,18},{10... | collective-permute-start | bytes 73736 | tf_op jit(solution)/shard_map/ppermute | solution.py:134
  6.0 0.5 %collective-permute-start = (f32[48,128]{1,0:T(8,128)}, f32[48,128]{1,0:T(8,128)S(1)}, u32[]{:S(2)}, u32[]{:S(2)}) collective-permute-start(f32[48,128]{1,0:T(8,128)} %bitcast.9), channel_id=1, source_target_pairs={{0,8},{8,0},{16,24},{24,16},{1,9},{9,1},{17,25},{25,17},{2,10},{10... | collective-permute-start | bytes 73736 | tf_op jit(solution)/shard_map/ppermute | solution.py:134
  6.5 0.5 %collective-permute-done.4.refs_6_ = f32[48,128]{1,0:T(8,128)S(1)} collective-permute-done((f32[48,128]{1,0:T(8,128)}, f32[48,128]{1,0:T(8,128)S(1)}, u32[]{:S(2)}, u32[]{:S(2)}) %collective-permute-start.4) | collective-permute-done | bytes 24608 | tf_op jit(solution)/shard_map/ppermute | solution.py:136
  7.1 0.0 copy-start
  7.1 1.2 %collective-permute-done.3.refs_5_ = f32[48,128]{1,0:T(8,128)S(1)} collective-permute-done((f32[48,128]{1,0:T(8,128)}, f32[48,128]{1,0:T(8,128)S(1)}, u32[]{:S(2)}, u32[]{:S(2)}) %collective-permute-start.3) | collective-permute-done | bytes 24608 | tf_op jit(solution)/shard_map/ppermute | solution.py:136
  8.3 0.0 copy-start.1
  8.3 0.0 collective-permute-done.2.refs_4_
  8.3 0.0 copy-start.2
  8.3 1.2 %collective-permute-done.1.refs_3_ = f32[48,128]{1,0:T(8,128)S(1)} collective-permute-done((f32[48,128]{1,0:T(8,128)}, f32[48,128]{1,0:T(8,128)S(1)}, u32[]{:S(2)}, u32[]{:S(2)}) %collective-permute-start.1) | collective-permute-done | bytes 24608 | tf_op jit(solution)/shard_map/ppermute | solution.py:134
  9.5 0.0 copy-start.3
  9.5 0.6 %collective-permute-done.refs_2_ = f32[48,128]{1,0:T(8,128)S(1)} collective-permute-done((f32[48,128]{1,0:T(8,128)}, f32[48,128]{1,0:T(8,128)S(1)}, u32[]{:S(2)}, u32[]{:S(2)}) %collective-permute-start) | collective-permute-done | bytes 24608 | tf_op jit(solution)/shard_map/ppermute | solution.py:134
  10.1 0.0 copy-done
  10.1 0.0 copy-done.1
  10.1 0.0 copy-done.2
  10.1 0.0 copy-done.3
  10.1 0.0 copy-start.4
  10.2 0.6 %copy-done.4 = f32[48,128]{1,0:T(8,128)} copy-done((f32[48,128]{1,0:T(8,128)}, f32[48,128]{1,0:T(8,128)S(1)}, u32[]{:S(2)}) %copy-start.4) | copy-done | bytes 24600
  10.7 2.3 %tiles.1 = f32[2,2,2]{2,1,0:T(2,128)} custom-call(s32[2,8]{1,0:T(2,128)} %refs_0_.1, f32[48,128]{1,0:T(8,128)} %bitcast.10, f32[48,128]{1,0:T(8,128)} %copy-done.4, f32[48,128]{1,0:T(8,128)} %copy-done.3, f32[48,128]{1,0:T(8,128)} %copy-done.2, f32[48,128]{1,0:T(8,128)} %copy-done.1, f32[48,128]{1,0:T(8,128)} %copy-done), custom_call_target="tpu_custom_call" | custom-call | tf_op jit(solution)/shard_map/tiles/pallas_call | solution.py:140
Async XLA Ops:
  0.0 7.1 %collective-permute-start.4 = (f32[48,128]{1,0:T(8,128)}, f32[48,128]{1,0:T(8,128)S(1)}, u32[]{:S(2)}, u32[]{:S(2)}) collective-permute-start(f32[48,128]{1,0:T(8,128)} %bitcast.5), channel_id=1, source_target_pairs={{0,2},{1,3},{2,4},{3,5},{4,6},{5,7},{6,0},{7,1},{8,10},{9,11},{10,... | collective-permute-start | bytes 73736 | tf_op jit(solution)/shard_map/ppermute | solution.py:136
  3.0 5.3 %collective-permute-start.3 = (f32[48,128]{1,0:T(8,128)}, f32[48,128]{1,0:T(8,128)S(1)}, u32[]{:S(2)}, u32[]{:S(2)}) collective-permute-start(f32[48,128]{1,0:T(8,128)} %bitcast.6), channel_id=1, source_target_pairs={{0,1},{1,2},{2,3},{3,4},{4,5},{5,6},{6,7},{7,0},{8,9},{9,10},{10,1... | collective-permute-start | bytes 73736 | tf_op jit(solution)/shard_map/ppermute | solution.py:136
  3.0 5.3 %collective-permute-start.2 = (f32[48,128]{1,0:T(8,128)}, f32[48,128]{1,0:T(8,128)S(1)}, u32[]{:S(2)}, u32[]{:S(2)}) collective-permute-start(f32[48,128]{1,0:T(8,128)} %bitcast.7), channel_id=1, source_target_pairs={{0,24},{8,16},{16,8},{24,0},{1,25},{9,17},{17,9},{25,1},{2,26},{10... | collective-permute-start | bytes 73736 | tf_op jit(solution)/shard_map/ppermute | solution.py:134
  5.5 4.0 %collective-permute-start.1 = (f32[48,128]{1,0:T(8,128)}, f32[48,128]{1,0:T(8,128)S(1)}, u32[]{:S(2)}, u32[]{:S(2)}) collective-permute-start(f32[48,128]{1,0:T(8,128)} %bitcast.8), channel_id=1, source_target_pairs={{0,16},{8,24},{16,0},{24,8},{1,17},{9,25},{17,1},{25,9},{2,18},{10... | collective-permute-start | bytes 73736 | tf_op jit(solution)/shard_map/ppermute | solution.py:134
  6.0 4.1 %collective-permute-start = (f32[48,128]{1,0:T(8,128)}, f32[48,128]{1,0:T(8,128)S(1)}, u32[]{:S(2)}, u32[]{:S(2)}) collective-permute-start(f32[48,128]{1,0:T(8,128)} %bitcast.9), channel_id=1, source_target_pairs={{0,8},{8,0},{16,24},{24,16},{1,9},{9,1},{17,25},{25,17},{2,10},{10... | collective-permute-start | bytes 73736 | tf_op jit(solution)/shard_map/ppermute | solution.py:134
  7.1 3.1 %copy-start = (f32[48,128]{1,0:T(8,128)}, f32[48,128]{1,0:T(8,128)S(1)}, u32[]{:S(2)}) copy-start(f32[48,128]{1,0:T(8,128)S(1)} %collective-permute-done.4.refs_6_) | copy-start | bytes 73732
  8.3 1.8 %copy-start.1 = (f32[48,128]{1,0:T(8,128)}, f32[48,128]{1,0:T(8,128)S(1)}, u32[]{:S(2)}) copy-start(f32[48,128]{1,0:T(8,128)S(1)} %collective-permute-done.3.refs_5_) | copy-start | bytes 73732
  8.3 1.8 %copy-start.2 = (f32[48,128]{1,0:T(8,128)}, f32[48,128]{1,0:T(8,128)S(1)}, u32[]{:S(2)}) copy-start(f32[48,128]{1,0:T(8,128)S(1)} %collective-permute-done.2.refs_4_) | copy-start | bytes 73732
  9.5 0.6 %copy-start.3 = (f32[48,128]{1,0:T(8,128)}, f32[48,128]{1,0:T(8,128)S(1)}, u32[]{:S(2)}) copy-start(f32[48,128]{1,0:T(8,128)S(1)} %collective-permute-done.1.refs_3_) | copy-start | bytes 73732
  10.1 0.6 %copy-start.4 = (f32[48,128]{1,0:T(8,128)}, f32[48,128]{1,0:T(8,128)S(1)}, u32[]{:S(2)}) copy-start(f32[48,128]{1,0:T(8,128)S(1)} %collective-permute-done.refs_2_) | copy-start | bytes 73732

commit v2 on v1

--- a/solution.py
+++ b/solution.py
@@ -143,7 +143,7 @@
         in_specs=[pl.BlockSpec(memory_space=pltpu.SMEM)] + [vmem] * (n_row + n_tiles),
         out_specs=vmem,
         name="tiles",
-    )(roots, *row_blocks, *col_blocks)
+    )(roots, packed, *[pltpu.with_memory_space_constraint(b, pltpu.VMEM) for b in row_blocks[1:] + col_blocks])
 
 
 def solution(mesh):

time: 13.3 us -> 12.5 us (0.940)
  local copies, waits for them, and re-layouts: 0.61 us -> 0 us
    unnamed x10 -> x0, local copies, waits for them, and re-layouts: 0.61 us -> none
where the time goes in v2:
time: 12.5 us; the launch traced here: 12.3 us
  starting transfers between devices  6.51 us (52%)
  waiting for transfers between devices  3.6 us (29%)
  Pallas kernels  2.19 us (18%)
    ppermute x3, starting transfers between devices, local(): row_blocks.append(lax.ppermute(packed, 'row', route))  3.49 us
    ppermute x2, starting transfers between devices, local(): lax.ppermute(packed, 'col', [(i, (i + s + 1) % n_col) for i in range(n_co...  3.03 us
    pallas_call x1, Pallas kernels, local(): pl.pallas_call(lambda *refs: kernel(powers, n_row, *refs), out_shape=jax....  2.19 us
    ppermute x3, waiting for transfers between devices, local(): row_blocks.append(lax.ppermute(packed, 'row', route))  1.84 us
    ppermute x2, waiting for transfers between devices, local(): lax.ppermute(packed, 'col', [(i, (i + s + 1) % n_col) for i in range(n_co...  1.77 us
  transfers between devices with their start and end apart: 5, of which 4 were waited for; matrix products, arithmetic and copies ran while one was open for 0% of the time, Pallas kernels for 0%

profile of v2, /device:TPU:0, one launch (start us, length us, event | category | flops | bytes accessed | tf_op | source)
XLA Modules:
  0.0 12.3 jit_solution(5035902084504160002)
XLA Ops:
  0.0 3.0 %collective-permute-start.4 = (f32[48,128]{1,0:T(8,128)}, f32[48,128]{1,0:T(8,128)S(1)}, u32[]{:S(2)}, u32[]{:S(2)}) collective-permute-start(f32[48,128]{1,0:T(8,128)} %bitcast.5), channel_id=1, source_target_pairs={{0,2},{1,3},{2,4},{3,5},{4,6},{5,7},{6,0},{7,1},{8,10},{9,11},{10,... | collective-permute-start | bytes 73736 | tf_op jit(solution)/shard_map/ppermute | solution.py:136
  3.0 0.0 collective-permute-start.3
  3.0 2.4 %collective-permute-start.2 = (f32[48,128]{1,0:T(8,128)}, f32[48,128]{1,0:T(8,128)S(1)}, u32[]{:S(2)}, u32[]{:S(2)}) collective-permute-start(f32[48,128]{1,0:T(8,128)} %bitcast.7), channel_id=1, source_target_pairs={{0,24},{8,16},{16,8},{24,0},{1,25},{9,17},{17,9},{25,1},{2,26},{10... | collective-permute-start | bytes 73736 | tf_op jit(solution)/shard_map/ppermute | solution.py:134
  5.5 0.5 %collective-permute-start.1 = (f32[48,128]{1,0:T(8,128)}, f32[48,128]{1,0:T(8,128)S(1)}, u32[]{:S(2)}, u32[]{:S(2)}) collective-permute-start(f32[48,128]{1,0:T(8,128)} %bitcast.8), channel_id=1, source_target_pairs={{0,16},{8,24},{16,0},{24,8},{1,17},{9,25},{17,1},{25,9},{2,18},{10... | collective-permute-start | bytes 73736 | tf_op jit(solution)/shard_map/ppermute | solution.py:134
  6.0 0.5 %collective-permute-start = (f32[48,128]{1,0:T(8,128)}, f32[48,128]{1,0:T(8,128)S(1)}, u32[]{:S(2)}, u32[]{:S(2)}) collective-permute-start(f32[48,128]{1,0:T(8,128)} %bitcast.9), channel_id=1, source_target_pairs={{0,8},{8,0},{16,24},{24,16},{1,9},{9,1},{17,25},{25,17},{2,10},{10... | collective-permute-start | bytes 73736 | tf_op jit(solution)/shard_map/ppermute | solution.py:134
  6.5 0.5 %collective-permute-done.4.refs_6_ = f32[48,128]{1,0:T(8,128)S(1)} collective-permute-done((f32[48,128]{1,0:T(8,128)}, f32[48,128]{1,0:T(8,128)S(1)}, u32[]{:S(2)}, u32[]{:S(2)}) %collective-permute-start.4) | collective-permute-done | bytes 24608 | tf_op jit(solution)/shard_map/ppermute | solution.py:136
  7.1 1.2 %collective-permute-done.3.refs_5_ = f32[48,128]{1,0:T(8,128)S(1)} collective-permute-done((f32[48,128]{1,0:T(8,128)}, f32[48,128]{1,0:T(8,128)S(1)}, u32[]{:S(2)}, u32[]{:S(2)}) %collective-permute-start.3) | collective-permute-done | bytes 24608 | tf_op jit(solution)/shard_map/ppermute | solution.py:136
  8.3 0.0 collective-permute-done.2.refs_4_
  8.3 1.2 %collective-permute-done.1.refs_3_ = f32[48,128]{1,0:T(8,128)S(1)} collective-permute-done((f32[48,128]{1,0:T(8,128)}, f32[48,128]{1,0:T(8,128)S(1)}, u32[]{:S(2)}, u32[]{:S(2)}) %collective-permute-start.1) | collective-permute-done | bytes 24608 | tf_op jit(solution)/shard_map/ppermute | solution.py:134
  9.5 0.6 %collective-permute-done.refs_2_ = f32[48,128]{1,0:T(8,128)S(1)} collective-permute-done((f32[48,128]{1,0:T(8,128)}, f32[48,128]{1,0:T(8,128)S(1)}, u32[]{:S(2)}, u32[]{:S(2)}) %collective-permute-start) | collective-permute-done | bytes 24608 | tf_op jit(solution)/shard_map/ppermute | solution.py:134
  10.1 2.2 %tiles.1 = f32[2,2,2]{2,1,0:T(2,128)} custom-call(s32[2,8]{1,0:T(2,128)} %refs_0_.1, f32[48,128]{1,0:T(8,128)} %bitcast.10, f32[48,128]{1,0:T(8,128)S(1)} %collective-permute-done.refs_2_, f32[48,128]{1,0:T(8,128)S(1)} %collective-permute-done.1.refs_3_, f32[48,128]{1,0:T(8,128)S(1)} %collective-permute-done.2.refs_4_, ...), custom_call_target="tpu_custom_call" | custom-call | tf_op jit(solution)/shard_map/tiles/pallas_call | solution.py:140
Async XLA Ops:
  0.0 7.1 %collective-permute-start.4 = (f32[48,128]{1,0:T(8,128)}, f32[48,128]{1,0:T(8,128)S(1)}, u32[]{:S(2)}, u32[]{:S(2)}) collective-permute-start(f32[48,128]{1,0:T(8,128)} %bitcast.5), channel_id=1, source_target_pairs={{0,2},{1,3},{2,4},{3,5},{4,6},{5,7},{6,0},{7,1},{8,10},{9,11},{10,... | collective-permute-start | bytes 73736 | tf_op jit(solution)/shard_map/ppermute | solution.py:136
  3.0 5.3 %collective-permute-start.3 = (f32[48,128]{1,0:T(8,128)}, f32[48,128]{1,0:T(8,128)S(1)}, u32[]{:S(2)}, u32[]{:S(2)}) collective-permute-start(f32[48,128]{1,0:T(8,128)} %bitcast.6), channel_id=1, source_target_pairs={{0,1},{1,2},{2,3},{3,4},{4,5},{5,6},{6,7},{7,0},{8,9},{9,10},{10,1... | collective-permute-start | bytes 73736 | tf_op jit(solution)/shard_map/ppermute | solution.py:136
  3.0 5.3 %collective-permute-start.2 = (f32[48,128]{1,0:T(8,128)}, f32[48,128]{1,0:T(8,128)S(1)}, u32[]{:S(2)}, u32[]{:S(2)}) collective-permute-start(f32[48,128]{1,0:T(8,128)} %bitcast.7), channel_id=1, source_target_pairs={{0,24},{8,16},{16,8},{24,0},{1,25},{9,17},{17,9},{25,1},{2,26},{10... | collective-permute-start | bytes 73736 | tf_op jit(solution)/shard_map/ppermute | solution.py:134
  5.5 4.0 %collective-permute-start.1 = (f32[48,128]{1,0:T(8,128)}, f32[48,128]{1,0:T(8,128)S(1)}, u32[]{:S(2)}, u32[]{:S(2)}) collective-permute-start(f32[48,128]{1,0:T(8,128)} %bitcast.8), channel_id=1, source_target_pairs={{0,16},{8,24},{16,0},{24,8},{1,17},{9,25},{17,1},{25,9},{2,18},{10... | collective-permute-start | bytes 73736 | tf_op jit(solution)/shard_map/ppermute | solution.py:134
  6.0 4.1 %collective-permute-start = (f32[48,128]{1,0:T(8,128)}, f32[48,128]{1,0:T(8,128)S(1)}, u32[]{:S(2)}, u32[]{:S(2)}) collective-permute-start(f32[48,128]{1,0:T(8,128)} %bitcast.9), channel_id=1, source_target_pairs={{0,8},{8,0},{16,24},{24,16},{1,9},{9,1},{17,25},{25,17},{2,10},{10... | collective-permute-start | bytes 73736 | tf_op jit(solution)/shard_map/ppermute | solution.py:134

commit v3 on v2

v3 whole, which is shorter than its diff:
```python
import math

import jax
import jax.numpy as jnp
import numpy as np
from jax import lax
from jax.experimental import pallas as pl
from jax.experimental.pallas import tpu as pltpu
from jax.sharding import PartitionSpec as P

WIDTH = 32
LANES = 128
DEPTH = 4

weight_var = 2.0
bias_var = 0.1


def remainder_coefficients(degree=6, nodes=64):
    u = 0.5 + 0.5 * np.cos(np.pi * (np.arange(nodes) + 0.5) / nodes)
    angle = 2.0 * np.arcsin(np.sqrt(0.5 * u))
    series = sum(
        (-1) ** n * 2.0 * n / math.factorial(2 * n + 1) * angle ** (2 * n + 1) * -1.0
        for n in range(1, 8)
    )
    exact = np.sin(angle) - angle * np.cos(angle)
    q = np.where(angle < 0.5, series, exact) / u**1.5
    fit = np.polynomial.chebyshev.Chebyshev.fit(u, q, degree, domain=[0.0, 1.0])
    return fit.convert(kind=np.polynomial.Polynomial).coef


COEFS = [float(v) / (2.0 * math.pi) for v in remainder_coefficients()]


class Stencil:
    def __init__(self, rows, block):
        self.rows, self.block = rows, block
        sub = lax.broadcasted_iota(jnp.int32, (rows, LANES), 0)
        lane = lax.broadcasted_iota(jnp.int32, (rows, LANES), 1)
        self.not_left = (lane % WIDTH) != 0
        self.not_right = (lane % WIDTH) != WIDTH - 1
        self.first_band = lane < WIDTH
        self.last_band = lane >= LANES - WIDTH
        self.above_inside = jnp.logical_and(self.first_band, sub >= block)
        self.below_inside = jnp.logical_and(self.last_band, sub < rows - block)
        self.even = (sub % 2) == 0
        self.sub, self.lane = sub, lane

    def box(self, m):
        left = jnp.where(self.not_left, pltpu.roll(m, 1, 1), 0.0)
        right = jnp.where(self.not_right, pltpu.roll(m, LANES - 1, 1), 0.0)
        across = m + left + right
        down = pltpu.roll(across, WIDTH, 1)
        up = pltpu.roll(across, LANES - WIDTH, 1)
        down_far = jnp.where(self.above_inside, pltpu.roll(down, self.block, 0), 0.0)
        up_far = jnp.where(self.below_inside, pltpu.roll(up, self.rows - self.block, 0), 0.0)
        return across + jnp.where(self.first_band, down_far, down) + jnp.where(self.last_band, up_far, up)

    def swapped(self, m):
        return jnp.where(self.even, pltpu.roll(m, self.rows - 1, 0), pltpu.roll(m, 1, 0))

    def channels(self, value):
        return [value[c * self.rows:(c + 1) * self.rows] for c in range(3)]

    def self_maps(self, value):
        energy = sum(v * v for v in self.channels(value))
        level = weight_var / 27.0 * self.box(energy) + bias_var
        levels = [level]
        for _ in range(DEPTH - 1):
            level = self.box(weight_var / 18.0 * level) + bias_var
            levels.append(level)
        inverse = [lax.rsqrt(v) for v in levels]
        return [v * r for v, r in zip(levels, inverse)], inverse


def prepare(powers, n_row, roots_ref, own_ref, *refs):
    n_tiles = roots_ref.shape[0]
    col_refs, (own_out, source_out, images_out, std_out, inv_out) = refs[:n_tiles], refs[n_tiles:]
    row_index, col_index = lax.axis_index("row"), lax.axis_index("col")
    block = own_ref.shape[0] // 24
    st = Stencil(8 * block, block)
    own_out[...] = own_ref[...]
    for s in range(n_tiles):
        root = roots_ref[s, col_index]
        source = root ^ row_index if powers else lax.rem(row_index - root + n_row, n_row)
        source_out[s] = jnp.full((8, LANES), source, jnp.int32)
        value = col_refs[s][...]
        std, inv = st.self_maps(value)
        for d in range(2):
            turn = st.swapped if d else lambda v: v
            for c, v in enumerate(st.channels(value)):
                images_out[s, d, c] = turn(v)
            for l in range(DEPTH):
                std_out[s, d, l] = turn(std[l])
                inv_out[s, d, l] = turn(inv[l])


def kernel(n_tiles, order, source_ref, images_ref, std_ref, inv_ref, *refs):
    row_refs, out_ref = refs[:-1], refs[-1]
    block = row_refs[0].shape[0] // 24
    st = Stencil(8 * block, block)

    def relu_map(k, scale, inverse):
        c = k * inverse
        u = jnp.maximum(1.0 - jnp.abs(c), 0.0)
        poly = jnp.full_like(u, COEFS[-1])
        for coef in COEFS[-2::-1]:
            poly = poly * u + coef
        return 0.5 * jnp.maximum(k, 0.0) + scale * (u * jnp.sqrt(u)) * poly

    sums = []
    for s in range(n_tiles):
        source = source_ref[s]
        row_value = row_refs[0][...].reshape(-1, 8, LANES)
        for n, k in enumerate(order, 1):
            row_value = jnp.where((source == k)[None], row_refs[n][...].reshape(-1, 8, LANES), row_value)
        row_value = row_value.reshape(-1, LANES)
        row_std, row_inv = st.self_maps(row_value)
        for d in range(2):
            cross = sum(a * images_ref[s, d, c] for c, a in enumerate(st.channels(row_value)))
            level = weight_var / 27.0 * st.box(cross) + bias_var
            for l in range(DEPTH):
                mapped = relu_map(level, row_std[l] * std_ref[s, d, l], row_inv[l] * inv_ref[s, d, l])
                if l < DEPTH - 1:
                    level = weight_var / 9.0 * st.box(mapped) + bias_var
            total = mapped[:8] + mapped[8:]
            total = total + pltpu.roll(total, 4, 0)
            sums.append(total + pltpu.roll(total, 2, 0))
    sub8 = st.sub[:8]
    packed = sums[0]
    for q in range(8):
        s, a, b = (q // 2) % 2, q % 2, q // 4
        packed = jnp.where(sub8 == q, sums[2 * s + (a ^ b)], packed)
    mean = jnp.sum(packed, axis=1, keepdims=True) * (1.0 / 1024.0)
    value = jnp.broadcast_to(weight_var * mean + bias_var, (8, LANES))
    result = jnp.where(st.lane[:8] == 0, value, pltpu.roll(value, 4, 0))
    for s in range(n_tiles):
        out_ref[s] = result[2 * s:2 * s + 2, 0:2]


def local(images, roots):
    n_row, n_col = lax.axis_size("row"), lax.axis_size("col")
    n_tiles = roots.shape[0]
    block, ch, pix = images.shape
    tiles = pix // LANES
    packed = images.reshape(block, ch, tiles, LANES).transpose(1, 2, 0, 3).reshape(ch * tiles * block, LANES)
    powers = n_row & (n_row - 1) == 0
    row_blocks = [packed]
    order = list(range(n_row - 1, 0, -1))
    for k in order:
        if powers:
            route = [(i, i ^ k) for i in range(n_row)]
        else:
            route = [(i, (i + k) % n_row) for i in range(n_row)]
        row_blocks.append(lax.ppermute(packed, "row", route))
    col_blocks = [
        lax.ppermute(packed, "col", [(i, (i + s + 1) % n_col) for i in range(n_col)])
        for s in range(n_tiles)
    ]
    vmem = pl.BlockSpec(memory_space=pltpu.VMEM)
    rows = 8 * block

    def placed(value):
        return pltpu.with_memory_space_constraint(value, pltpu.VMEM)

    own, *made = pl.pallas_call(
        lambda *refs: prepare(powers, n_row, *refs),
        out_shape=[
            pltpu.VMEM(packed.shape, jnp.float32),
            pltpu.VMEM((n_tiles, 8, LANES), jnp.int32),
            pltpu.VMEM((n_tiles, 2, ch, rows, LANES), jnp.float32),
            pltpu.VMEM((n_tiles, 2, DEPTH, rows, LANES), jnp.float32),
            pltpu.VMEM((n_tiles, 2, DEPTH, rows, LANES), jnp.float32),
        ],
        in_specs=[pl.BlockSpec(memory_space=pltpu.SMEM)] + [vmem] * (1 + n_tiles),
        out_specs=[vmem] * 5,
        name="prepare",
    )(roots, packed, *map(placed, col_blocks))
    return pl.pallas_call(
        lambda *refs: kernel(n_tiles, order, *refs),
        out_shape=jax.ShapeDtypeStruct((n_tiles, block, block), jnp.float32),
        in_specs=[vmem] * (4 + n_row),
        out_specs=vmem,
        name="tiles",
    )(*map(placed, made), placed(own), *map(placed, row_blocks[1:]))


def solution(mesh):
    in_specs = (P(("row", "col"), None, None), P())
    out_specs = P(None, "row", "col")
    return jax.shard_map(local, mesh=mesh, in_specs=in_specs, out_specs=out_specs, check_vma=False)
```

time: 12.5 us -> 11.8 us (0.944)
  waiting for transfers between devices: 3.6 us -> 2.23 us
  Pallas kernels: 2.19 us -> 2.83 us
    ppermute x2, waiting for transfers between devices: 1.77 us -> 0.52 us  [local(): lax.ppermute(packed, 'col', [(i, (i + s + 1) % n_col) for i in range(n_co...]
    pallas_call x1 -> x2, Pallas kernels: 2.19 us -> 2.83 us  [the longest x1 1.46 us: local(): pl.pallas_call(lambda *refs: kernel(n_tiles, order, *refs), out_shape=jax...]
  transfers between devices with their start and end apart: 5 -> 5, of which waited for: 4 -> 3; matrix products, arithmetic and copies ran while one was open for 0% -> 0% of each run, Pallas kernels for 0% -> 12%
where the time goes in v3:
time: 11.8 us; the launch traced here: 11.6 us
  starting transfers between devices  6.55 us (56%)
  Pallas kernels  2.83 us (24%)
  waiting for transfers between devices  2.23 us (19%)
    ppermute x3, starting transfers between devices, local(): row_blocks.append(lax.ppermute(packed, 'row', route))  3.49 us
    ppermute x2, starting transfers between devices, local(): lax.ppermute(packed, 'col', [(i, (i + s + 1) % n_col) for i in range(n_co...  3.06 us
    ppermute x3, waiting for transfers between devices, local(): row_blocks.append(lax.ppermute(packed, 'row', route))  1.71 us
    pallas_call x1, Pallas kernels, local(): pl.pallas_call(lambda *refs: kernel(n_tiles, order, *refs), out_shape=jax...  1.46 us
    pallas_call x1, Pallas kernels, local(): pl.pallas_call(lambda *refs: prepare(powers, n_row, *refs), out_shape=[pl...  1.37 us
    ppermute x2, waiting for transfers between devices, local(): lax.ppermute(packed, 'col', [(i, (i + s + 1) % n_col) for i in range(n_co...  0.52 us
  transfers between devices with their start and end apart: 5, of which 3 were waited for; matrix products, arithmetic and copies ran while one was open for 0% of the time, Pallas kernels for 12%

profile of v3, /device:TPU:0, one launch (start us, length us, event | category | flops | bytes accessed | tf_op | source)
XLA Modules:
  0.0 11.6 jit_solution(8779209232142544005)
XLA Ops:
  0.0 0.5 %collective-permute-start = (f32[48,128]{1,0:T(8,128)}, f32[48,128]{1,0:T(8,128)S(1)}, u32[]{:S(2)}, u32[]{:S(2)}) collective-permute-start(f32[48,128]{1,0:T(8,128)} %bitcast.5), channel_id=1, source_target_pairs={{0,1},{1,2},{2,3},{3,4},{4,5},{5,6},{6,7},{7,0},{8,9},{9,10},{10,1... | collective-permute-start | bytes 73736 | tf_op jit(solution)/shard_map/ppermute | solution.py:157
  0.5 2.6 %collective-permute-start.1 = (f32[48,128]{1,0:T(8,128)}, f32[48,128]{1,0:T(8,128)S(1)}, u32[]{:S(2)}, u32[]{:S(2)}) collective-permute-start(f32[48,128]{1,0:T(8,128)} %bitcast.6), channel_id=1, source_target_pairs={{0,2},{1,3},{2,4},{3,5},{4,6},{5,7},{6,0},{7,1},{8,10},{9,11},{10,... | collective-permute-start | bytes 73736 | tf_op jit(solution)/shard_map/ppermute | solution.py:157
  3.1 2.4 %collective-permute-start.2 = (f32[48,128]{1,0:T(8,128)}, f32[48,128]{1,0:T(8,128)S(1)}, u32[]{:S(2)}, u32[]{:S(2)}) collective-permute-start(f32[48,128]{1,0:T(8,128)} %bitcast.7), channel_id=1, source_target_pairs={{0,24},{8,16},{16,8},{24,0},{1,25},{9,17},{17,9},{25,1},{2,26},{10... | collective-permute-start | bytes 73736 | tf_op jit(solution)/shard_map/ppermute | solution.py:155
  5.5 0.5 %collective-permute-start.3 = (f32[48,128]{1,0:T(8,128)}, f32[48,128]{1,0:T(8,128)S(1)}, u32[]{:S(2)}, u32[]{:S(2)}) collective-permute-start(f32[48,128]{1,0:T(8,128)} %bitcast.8), channel_id=1, source_target_pairs={{0,16},{8,24},{16,0},{24,8},{1,17},{9,25},{17,1},{25,9},{2,18},{10... | collective-permute-start | bytes 73736 | tf_op jit(solution)/shard_map/ppermute | solution.py:155
  6.0 0.5 %collective-permute-start.4 = (f32[48,128]{1,0:T(8,128)}, f32[48,128]{1,0:T(8,128)S(1)}, u32[]{:S(2)}, u32[]{:S(2)}) collective-permute-start(f32[48,128]{1,0:T(8,128)} %bitcast.9), channel_id=1, source_target_pairs={{0,8},{8,0},{16,24},{24,16},{1,9},{9,1},{17,25},{25,17},{2,10},{10... | collective-permute-start | bytes 73736 | tf_op jit(solution)/shard_map/ppermute | solution.py:155
  6.5 0.0 collective-permute-done.refs_2_
  6.6 0.5 %collective-permute-done.1.refs_3_ = f32[48,128]{1,0:T(8,128)S(1)} collective-permute-done((f32[48,128]{1,0:T(8,128)}, f32[48,128]{1,0:T(8,128)S(1)}, u32[]{:S(2)}, u32[]{:S(2)}) %collective-permute-start.1) | collective-permute-done | bytes 24608 | tf_op jit(solution)/shard_map/ppermute | solution.py:157
  7.1 1.4 %prepare.1 = (f32[48,128]{1,0:T(8,128)S(1)}, s32[2,8,128]{2,1,0:T(8,128)S(1)}, f32[2,2,3,16,128]{4,3,2,1,0:T(8,128)S(1)}, f32[2,2,4,16,128]{4,3,2,1,0:T(8,128)S(1)}, f32[2,2,4,16,128]{4,3,2,1,0:T(8,128)S(1)}) custom-call(s32[2,8]{1,0:T(2,128)} %refs_0_.1, f32[48,128]{1,0:T(8,128)} %bitcast.10, f32[48,128]{1,0:T(8,128)S(1)} %collective-permute-done.refs_2_, ...), custom_call_target="tpu_custom_call" | custom-call | tf_op jit(solution)/shard_map/prepare/pallas_call | solution.py:166
  8.4 0.0 collective-permute-done.2.refs_5_
  8.5 1.2 %collective-permute-done.3.refs_6_ = f32[48,128]{1,0:T(8,128)S(1)} collective-permute-done((f32[48,128]{1,0:T(8,128)}, f32[48,128]{1,0:T(8,128)S(1)}, u32[]{:S(2)}, u32[]{:S(2)}) %collective-permute-start.3) | collective-permute-done | bytes 24608 | tf_op jit(solution)/shard_map/ppermute | solution.py:155
  9.7 0.5 %collective-permute-done.4.refs_7_ = f32[48,128]{1,0:T(8,128)S(1)} collective-permute-done((f32[48,128]{1,0:T(8,128)}, f32[48,128]{1,0:T(8,128)S(1)}, u32[]{:S(2)}, u32[]{:S(2)}) %collective-permute-start.4) | collective-permute-done | bytes 24608 | tf_op jit(solution)/shard_map/ppermute | solution.py:155
  10.2 1.5 %tiles.1 = f32[2,2,2]{2,1,0:T(2,128)} custom-call(s32[2,8,128]{2,1,0:T(8,128)S(1)} %get-tuple-element.10.refs_0_, f32[2,2,3,16,128]{4,3,2,1,0:T(8,128)S(1)} %get-tuple-element.11.refs_1_, f32[2,2,4,16,128]{4,3,2,1,0:T(8,128)S(1)} %get-tuple-element.12.refs_2_, f32[2,2,4,16,128]{4,3,2,1,0:T(8,128)S(1)} %get-tuple-element.13.refs_3_, ...), custom_call_target="tpu_custom_call" | custom-call | tf_op jit(solution)/shard_map/tiles/pallas_call | solution.py:179
Async XLA Ops:
  0.0 6.6 %collective-permute-start = (f32[48,128]{1,0:T(8,128)}, f32[48,128]{1,0:T(8,128)S(1)}, u32[]{:S(2)}, u32[]{:S(2)}) collective-permute-start(f32[48,128]{1,0:T(8,128)} %bitcast.5), channel_id=1, source_target_pairs={{0,1},{1,2},{2,3},{3,4},{4,5},{5,6},{6,7},{7,0},{8,9},{9,10},{10,1... | collective-permute-start | bytes 73736 | tf_op jit(solution)/shard_map/ppermute | solution.py:157
  0.5 6.6 %collective-permute-start.1 = (f32[48,128]{1,0:T(8,128)}, f32[48,128]{1,0:T(8,128)S(1)}, u32[]{:S(2)}, u32[]{:S(2)}) collective-permute-start(f32[48,128]{1,0:T(8,128)} %bitcast.6), channel_id=1, source_target_pairs={{0,2},{1,3},{2,4},{3,5},{4,6},{5,7},{6,0},{7,1},{8,10},{9,11},{10,... | collective-permute-start | bytes 73736 | tf_op jit(solution)/shard_map/ppermute | solution.py:157
  3.1 5.4 %collective-permute-start.2 = (f32[48,128]{1,0:T(8,128)}, f32[48,128]{1,0:T(8,128)S(1)}, u32[]{:S(2)}, u32[]{:S(2)}) collective-permute-start(f32[48,128]{1,0:T(8,128)} %bitcast.7), channel_id=1, source_target_pairs={{0,24},{8,16},{16,8},{24,0},{1,25},{9,17},{17,9},{25,1},{2,26},{10... | collective-permute-start | bytes 73736 | tf_op jit(solution)/shard_map/ppermute | solution.py:155
  5.5 4.2 %collective-permute-start.3 = (f32[48,128]{1,0:T(8,128)}, f32[48,128]{1,0:T(8,128)S(1)}, u32[]{:S(2)}, u32[]{:S(2)}) collective-permute-start(f32[48,128]{1,0:T(8,128)} %bitcast.8), channel_id=1, source_target_pairs={{0,16},{8,24},{16,0},{24,8},{1,17},{9,25},{17,1},{25,9},{2,18},{10... | collective-permute-start | bytes 73736 | tf_op jit(solution)/shard_map/ppermute | solution.py:155
  6.0 4.1 %collective-permute-start.4 = (f32[48,128]{1,0:T(8,128)}, f32[48,128]{1,0:T(8,128)S(1)}, u32[]{:S(2)}, u32[]{:S(2)}) collective-permute-start(f32[48,128]{1,0:T(8,128)} %bitcast.9), channel_id=1, source_target_pairs={{0,8},{8,0},{16,24},{24,16},{1,9},{9,1},{17,25},{25,17},{2,10},{10... | collective-permute-start | bytes 73736 | tf_op jit(solution)/shard_map/ppermute | solution.py:155

commit v4 on v3

--- a/solution.py
+++ b/solution.py
@@ -73,32 +73,45 @@
         return [v * r for v, r in zip(levels, inverse)], inverse
 
 
-def prepare(powers, n_row, roots_ref, own_ref, *refs):
+def prepare(powers, n_row, roots_ref, own_ref, near_ref, far_ref, own_out, pick_out, near_out, far_out, std_out, inv_out):
     n_tiles = roots_ref.shape[0]
-    col_refs, (own_out, source_out, images_out, std_out, inv_out) = refs[:n_tiles], refs[n_tiles:]
     row_index, col_index = lax.axis_index("row"), lax.axis_index("col")
     block = own_ref.shape[0] // 24
     st = Stencil(8 * block, block)
     own_out[...] = own_ref[...]
+    near_out[...] = near_ref[...]
     for s in range(n_tiles):
         root = roots_ref[s, col_index]
         source = root ^ row_index if powers else lax.rem(row_index - root + n_row, n_row)
-        source_out[s] = jnp.full((8, LANES), source, jnp.int32)
-        value = col_refs[s][...]
-        std, inv = st.self_maps(value)
-        for d in range(2):
-            turn = st.swapped if d else lambda v: v
-            for c, v in enumerate(st.channels(value)):
-                images_out[s, d, c] = turn(v)
-            for l in range(DEPTH):
-                std_out[s, d, l] = turn(std[l])
-                inv_out[s, d, l] = turn(inv[l])
-
-
-def kernel(n_tiles, order, source_ref, images_ref, std_ref, inv_ref, *refs):
+        pick_out[s] = jnp.full((8, LANES), source, jnp.int32)
+    pick_out[n_tiles] = jnp.full((8, LANES), lax.rem(col_index, 2), jnp.int32)
+    value = far_ref[...]
+    std, inv = st.self_maps(value)
+    for d in range(2):
+        turn = st.swapped if d else lambda v: v
+        for c, v in enumerate(st.channels(value)):
+            far_out[d, c] = turn(v)
+        for l in range(DEPTH):
+            std_out[d, l] = turn(std[l])
+            inv_out[d, l] = turn(inv[l])
+
+
+def kernel(n_tiles, order, pick_ref, near_ref, far_ref, std_ref, inv_ref, passed_ref, *refs):
     row_refs, out_ref = refs[:-1], refs[-1]
     block = row_refs[0].shape[0] // 24
     st = Stencil(8 * block, block)
+
+    def chosen(flags, first, second):
+        first, second = first.reshape(-1, 8, LANES), second.reshape(-1, 8, LANES)
+        return jnp.where(flags[None], first, second).reshape(-1, LANES)
+
+    odd = pick_ref[n_tiles] == 1
+    near = chosen(odd, near_ref[...], passed_ref[...])
+    near_std, near_inv = st.self_maps(near)
+    columns = [
+        [(st.channels(near), near_std, near_inv)] + [tuple([st.swapped(v) for v in part] for part in (st.channels(near), near_std, near_inv))],
+        [([far_ref[d, c] for c in range(3)], [std_ref[d, l] for l in range(DEPTH)], [inv_ref[d, l] for l in range(DEPTH)]) for d in range(2)],
+    ]
 
     def relu_map(k, scale, inverse):
         c = k * inverse
@@ -110,17 +123,17 @@
 
     sums = []
     for s in range(n_tiles):
-        source = source_ref[s]
-        row_value = row_refs[0][...].reshape(-1, 8, LANES)
+        source = pick_ref[s]
+        row_value = row_refs[0][...]
         for n, k in enumerate(order, 1):
-            row_value = jnp.where((source == k)[None], row_refs[n][...].reshape(-1, 8, LANES), row_value)
-        row_value = row_value.reshape(-1, LANES)
+            row_value = chosen(source == k, row_refs[n][...], row_value)
         row_std, row_inv = st.self_maps(row_value)
         for d in range(2):
-            cross = sum(a * images_ref[s, d, c] for c, a in enumerate(st.channels(row_value)))
+            images, col_std, col_inv = columns[s][d]
+            cross = sum(a * b for a, b in zip(st.channels(row_value), images))
             level = weight_var / 27.0 * st.box(cross) + bias_var
             for l in range(DEPTH):
-                mapped = relu_map(level, row_std[l] * std_ref[s, d, l], row_inv[l] * inv_ref[s, d, l])
+                mapped = relu_map(level, row_std[l] * col_std[l], row_inv[l] * col_inv[l])
                 if l < DEPTH - 1:
                     level = weight_var / 9.0 * st.box(mapped) + bias_var
             total = mapped[:8] + mapped[8:]
@@ -145,44 +158,54 @@
     tiles = pix // LANES
     packed = images.reshape(block, ch, tiles, LANES).transpose(1, 2, 0, 3).reshape(ch * tiles * block, LANES)
     powers = n_row & (n_row - 1) == 0
-    row_blocks = [packed]
-    order = list(range(n_row - 1, 0, -1))
+    def moved(value, shift):
+        pairs = []
+        for i in range(n_row):
+            for j in range(n_col):
+                row, col = shift(i, j)
+                pairs.append((i * n_col + j, row * n_col + col))
+        return lax.ppermute(value, ("row", "col"), pairs)
+
+    def row_shift(k, crossed):
+        def shift(i, j):
+            return (i ^ k if powers else (i + k) % n_row), (j ^ 1 if crossed else j)
+        return shift
+
+    near = moved(packed, lambda i, j: (i, j ^ 1))
+    far = moved(packed, lambda i, j: (i, (j + 2) % n_col))
+    order = [k for k in range(n_row - 1, 0, -1) if k % 2 == 0] + [k for k in range(n_row - 1, 0, -1) if k % 2]
+    row_blocks = []
     for k in order:
-        if powers:
-            route = [(i, i ^ k) for i in range(n_row)]
-        else:
-            route = [(i, (i + k) % n_row) for i in range(n_row)]
-        row_blocks.append(lax.ppermute(packed, "row", route))
-    col_blocks = [
-        lax.ppermute(packed, "col", [(i, (i + s + 1) % n_col) for i in range(n_col)])
-        for s in range(n_tiles)
-    ]
+        crossed = k % 2 == 1
+        row_blocks.append(moved(near if crossed else packed, row_shift(k, crossed)))
+    passed = moved(far, lambda i, j: (i, j ^ 1))
     vmem = pl.BlockSpec(memory_space=pltpu.VMEM)
     rows = 8 * block
 
     def placed(value):
         return pltpu.with_memory_space_constraint(value, pltpu.VMEM)
 
-    own, *made = pl.pallas_call(
+    own, pick, near_copy, *made = pl.pallas_call(
         lambda *refs: prepare(powers, n_row, *refs),
         out_shape=[
             pltpu.VMEM(packed.shape, jnp.float32),
-            pltpu.VMEM((n_tiles, 8, LANES), jnp.int32),
-            pltpu.VMEM((n_tiles, 2, ch, rows, LANES), jnp.float32),
-            pltpu.VMEM((n_tiles, 2, DEPTH, rows, LANES), jnp.float32),
-            pltpu.VMEM((n_tiles, 2, DEPTH, rows, LANES), jnp.float32),
+            pltpu.VMEM((n_tiles + 1, 8, LANES), jnp.int32),
+            pltpu.VMEM(packed.shape, jnp.float32),
+            pltpu.VMEM((2, ch, rows, LANES), jnp.float32),
+            pltpu.VMEM((2, DEPTH, rows, LANES), jnp.float32),
+            pltpu.VMEM((2, DEPTH, rows, LANES), jnp.float32),
         ],
-        in_specs=[pl.BlockSpec(memory_space=pltpu.SMEM)] + [vmem] * (1 + n_tiles),
-        out_specs=[vmem] * 5,
+        in_specs=[pl.BlockSpec(memory_space=pltpu.SMEM)] + [vmem] * 3,
+        out_specs=[vmem] * 6,
         name="prepare",
-    )(roots, packed, *map(placed, col_blocks))
+    )(roots, packed, placed(near), placed(far))
     return pl.pallas_call(
         lambda *refs: kernel(n_tiles, order, *refs),
         out_shape=jax.ShapeDtypeStruct((n_tiles, block, block), jnp.float32),
-        in_specs=[vmem] * (4 + n_row),
+        in_specs=[vmem] * (7 + n_row - 1),
         out_specs=vmem,
         name="tiles",
-    )(*map(placed, made), placed(own), *map(placed, row_blocks[1:]))
+    )(*map(placed, [pick, near_copy, *made, passed, own, *row_blocks]))
 
 
 def solution(mesh):

time: 11.8 us -> 10.5 us (0.89)
  the two profiles are of different devices: /device:TPU:0 before, /device:TPU:1 now
where the time goes in v4:
time: 10.5 us; the launch traced here: 10.4 us
  starting transfers between devices  6.31 us (60%)
  Pallas kernels  2.79 us (27%)
  waiting for transfers between devices  1.23 us (12%)
    ppermute x6, starting transfers between devices, moved(): return lax.ppermute(value, ('row', 'col'), pairs)  6.31 us
    pallas_call x1, Pallas kernels, local(): pl.pallas_call(lambda *refs: kernel(n_tiles, order, *refs), out_shape=jax...  1.46 us
    pallas_call x1, Pallas kernels, local(): pl.pallas_call(lambda *refs: prepare(powers, n_row, *refs), out_shape=[pl...  1.34 us
    ppermute x6, waiting for transfers between devices, moved(): return lax.ppermute(value, ('row', 'col'), pairs)  1.23 us
  transfers between devices with their start and end apart: 6, of which 2 were waited for; matrix products, arithmetic and copies ran while one was open for 0% of the time, Pallas kernels for 13%

profile of v4, /device:TPU:1, one launch (start us, length us, event | category | flops | bytes accessed | tf_op | source)
XLA Modules:
  0.0 10.4 jit_solution(17409933728960624312)
XLA Ops:
  0.0 0.1 collective-permute-start
  0.1 2.7 %collective-permute-start.1 = (f32[48,128]{1,0:T(8,128)}, f32[48,128]{1,0:T(8,128)S(1)}, u32[]{:S(2)}, u32[]{:S(2)}) collective-permute-start(f32[48,128]{1,0:T(8,128)} %bitcast.6), channel_id=1, source_target_pairs={{0,2},{1,3},{2,4},{3,5},{4,6},{5,7},{6,0},{7,1},{8,10},{9,11},{10,... | collective-permute-start | bytes 73736 | tf_op jit(solution)/shard_map/ppermute | solution.py:167
  2.8 1.2 %collective-permute-start.3 = (f32[48,128]{1,0:T(8,128)}, f32[48,128]{1,0:T(8,128)S(1)}, u32[]{:S(2)}, u32[]{:S(2)}) collective-permute-start(f32[48,128]{1,0:T(8,128)} %bitcast.7), channel_id=1, source_target_pairs={{0,16},{1,17},{2,18},{3,19},{4,20},{5,21},{6,22},{7,23},{8,24},{9,... | collective-permute-start | bytes 73736 | tf_op jit(solution)/shard_map/ppermute | solution.py:167
  4.0 0.0 collective-permute-done.refs_2_
  4.0 1.6 %collective-permute-start.4 = (f32[48,128]{1,0:T(8,128)S(1)}, f32[48,128]{1,0:T(8,128)S(1)}, u32[]{:S(2)}, u32[]{:S(2)}) collective-permute-start(f32[48,128]{1,0:T(8,128)S(1)} %collective-permute-done.refs_2_), channel_id=1, source_target_pairs={{0,25},{1,24},{2,27},{3,26},{4,29},{5,28},{6,31},{7,30},{8,17},{9,... | collective-permute-start | bytes 73736 | tf_op jit(solution)/shard_map/ppermute | solution.py:167
  5.6 0.1 collective-permute-start.5
  5.7 0.9 %collective-permute-done.1.refs_3_ = f32[48,128]{1,0:T(8,128)S(1)} collective-permute-done((f32[48,128]{1,0:T(8,128)}, f32[48,128]{1,0:T(8,128)S(1)}, u32[]{:S(2)}, u32[]{:S(2)}) %collective-permute-start.1) | collective-permute-done | bytes 24608 | tf_op jit(solution)/shard_map/ppermute | solution.py:167
  6.6 0.6 %collective-permute-start.2 = (f32[48,128]{1,0:T(8,128)S(1)}, f32[48,128]{1,0:T(8,128)S(1)}, u32[]{:S(2)}, u32[]{:S(2)}) collective-permute-start(f32[48,128]{1,0:T(8,128)S(1)} %collective-permute-done.1.refs_3_), channel_id=1, source_target_pairs={{0,1},{1,0},{2,3},{3,2},{4,5},{5,4},{6,7},{7,6},{8,9},{9,8},{10,11... | collective-permute-start | bytes 73736 | tf_op jit(solution)/shard_map/ppermute | solution.py:167
  7.2 1.3 %prepare.1 = (f32[48,128]{1,0:T(8,128)S(1)}, s32[3,8,128]{2,1,0:T(8,128)S(1)}, f32[48,128]{1,0:T(8,128)S(1)}, f32[2,3,16,128]{3,2,1,0:T(8,128)S(1)}, f32[2,4,16,...) custom-call(s32[2,8]{1,0:T(2,128)} %refs_0_.1, f32[48,128]{1,0:T(8,128)} %bitcast.8, ...), custom_call_target="tpu_custom_call" | custom-call | tf_op jit(solution)/shard_map/prepare/pallas_call | solution.py:188
  8.6 0.0 collective-permute-done.3.refs_7_
  8.6 0.0 collective-permute-done.4.refs_8_
  8.6 0.3 %collective-permute-done.5.refs_9_ = f32[48,128]{1,0:T(8,128)S(1)} collective-permute-done((f32[48,128]{1,0:T(8,128)S(1)}, f32[48,128]{1,0:T(8,128)S(1)}, u32[]{:S(2)}, u32[]{:S(2)}) %collective-permute-start.5) | collective-permute-done | bytes 24608 | tf_op jit(solution)/shard_map/ppermute | solution.py:167
  8.9 0.0 collective-permute-done.2.refs_5_
  8.9 1.5 %tiles.1 = f32[2,2,2]{2,1,0:T(2,128)} custom-call(s32[3,8,128]{2,1,0:T(8,128)S(1)} %get-tuple-element.11.refs_0_, f32[48,128]{1,0:T(8,128)S(1)} %get-tuple-element.12.refs_1_, f32[2,3,16,128]{3,2,1,0:T(8,128)S(1)} %get-tuple-element.13.refs_2_, f32[2,4,16,128]{3,2,1,0:T(8,128)S(1)} %get-tuple-element.14.refs_3_, ...), custom_call_target="tpu_custom_call" | custom-call | tf_op jit(solution)/shard_map/tiles/pallas_call | solution.py:202
Async XLA Ops:
  0.0 4.0 %collective-permute-start = (f32[48,128]{1,0:T(8,128)}, f32[48,128]{1,0:T(8,128)S(1)}, u32[]{:S(2)}, u32[]{:S(2)}) collective-permute-start(f32[48,128]{1,0:T(8,128)} %bitcast.5), channel_id=1, source_target_pairs={{0,1},{1,0},{2,3},{3,2},{4,5},{5,4},{6,7},{7,6},{8,9},{9,8},{10,11... | collective-permute-start | bytes 73736 | tf_op jit(solution)/shard_map/ppermute | solution.py:167
  0.1 6.6 %collective-permute-start.1 = (f32[48,128]{1,0:T(8,128)}, f32[48,128]{1,0:T(8,128)S(1)}, u32[]{:S(2)}, u32[]{:S(2)}) collective-permute-start(f32[48,128]{1,0:T(8,128)} %bitcast.6), channel_id=1, source_target_pairs={{0,2},{1,3},{2,4},{3,5},{4,6},{5,7},{6,0},{7,1},{8,10},{9,11},{10,... | collective-permute-start | bytes 73736 | tf_op jit(solution)/shard_map/ppermute | solution.py:167
  2.8 5.8 %collective-permute-start.3 = (f32[48,128]{1,0:T(8,128)}, f32[48,128]{1,0:T(8,128)S(1)}, u32[]{:S(2)}, u32[]{:S(2)}) collective-permute-start(f32[48,128]{1,0:T(8,128)} %bitcast.7), channel_id=1, source_target_pairs={{0,16},{1,17},{2,18},{3,19},{4,20},{5,21},{6,22},{7,23},{8,24},{9,... | collective-permute-start | bytes 73736 | tf_op jit(solution)/shard_map/ppermute | solution.py:167
  4.0 4.5 %collective-permute-start.4 = (f32[48,128]{1,0:T(8,128)S(1)}, f32[48,128]{1,0:T(8,128)S(1)}, u32[]{:S(2)}, u32[]{:S(2)}) collective-permute-start(f32[48,128]{1,0:T(8,128)S(1)} %collective-permute-done.refs_2_), channel_id=1, source_target_pairs={{0,25},{1,24},{2,27},{3,26},{4,29},{5,28},{6,31},{7,30},{8,17},{9,... | collective-permute-start | bytes 73736 | tf_op jit(solution)/shard_map/ppermute | solution.py:167
  5.6 3.3 %collective-permute-start.5 = (f32[48,128]{1,0:T(8,128)S(1)}, f32[48,128]{1,0:T(8,128)S(1)}, u32[]{:S(2)}, u32[]{:S(2)}) collective-permute-start(f32[48,128]{1,0:T(8,128)S(1)} %collective-permute-done.refs_2_), channel_id=1, source_target_pairs={{0,9},{1,8},{2,11},{3,10},{4,13},{5,12},{6,15},{7,14},{8,1},{9,0},... | collective-permute-start | bytes 73736 | tf_op jit(solution)/shard_map/ppermute | solution.py:167
  6.6 2.3 %collective-permute-start.2 = (f32[48,128]{1,0:T(8,128)S(1)}, f32[48,128]{1,0:T(8,128)S(1)}, u32[]{:S(2)}, u32[]{:S(2)}) collective-permute-start(f32[48,128]{1,0:T(8,128)S(1)} %collective-permute-done.1.refs_3_), channel_id=1, source_target_pairs={{0,1},{1,0},{2,3},{3,2},{4,5},{5,4},{6,7},{7,6},{8,9},{9,8},{10,11... | collective-permute-start | bytes 73736 | tf_op jit(solution)/shard_map/ppermute | solution.py:167

commit v5 on v4

v5 whole, which is shorter than its diff:
```python
import math

import jax
import jax.numpy as jnp
import numpy as np
from jax import lax
from jax.experimental import pallas as pl
from jax.experimental.pallas import tpu as pltpu
from jax.sharding import PartitionSpec as P

WIDTH = 32
LANES = 128
DEPTH = 4

weight_var = 2.0
bias_var = 0.1


def remainder_coefficients(degree=6, nodes=64):
    u = 0.5 + 0.5 * np.cos(np.pi * (np.arange(nodes) + 0.5) / nodes)
    angle = 2.0 * np.arcsin(np.sqrt(0.5 * u))
    series = sum(
        (-1) ** n * 2.0 * n / math.factorial(2 * n + 1) * angle ** (2 * n + 1) * -1.0
        for n in range(1, 8)
    )
    exact = np.sin(angle) - angle * np.cos(angle)
    q = np.where(angle < 0.5, series, exact) / u**1.5
    fit = np.polynomial.chebyshev.Chebyshev.fit(u, q, degree, domain=[0.0, 1.0])
    return fit.convert(kind=np.polynomial.Polynomial).coef


COEFS = [float(v) / (2.0 * math.pi) for v in remainder_coefficients()]


def prepare(powers, n_row, roots_ref, own_ref, near_ref, far_ref, own_out, pick_out, near_out, far_out):
    n_tiles = roots_ref.shape[0]
    row_index, col_index = lax.axis_index("row"), lax.axis_index("col")
    own_out[...] = own_ref[...]
    near_out[...] = near_ref[...]
    far_out[...] = far_ref[...]
    for s in range(n_tiles):
        root = roots_ref[s, col_index]
        source = root ^ row_index if powers else lax.rem(row_index - root + n_row, n_row)
        pick_out[s] = jnp.full((8, LANES), source, jnp.int32)
    pick_out[n_tiles] = jnp.full((8, LANES), lax.rem(col_index, 2), jnp.int32)


def kernel(n_tiles, order, pick_ref, near_ref, far_ref, passed_ref, *refs):
    row_refs, out_ref = refs[:-1], refs[-1]
    block = row_refs[0].shape[0] // 24
    rows, bands = 8 * block, LANES // WIDTH
    sub = lax.broadcasted_iota(jnp.int32, (rows, LANES), 0)
    lane = lax.broadcasted_iota(jnp.int32, (rows, LANES), 1)
    not_left, not_right = (lane % WIDTH) != 0, (lane % WIDTH) != WIDTH - 1
    first_rows, last_rows = sub < block, sub >= rows - block
    even = (sub % 2) == 0
    group = lane // WIDTH
    other_image = (group % 2) == 1

    def box(maps):
        before = jnp.where(first_rows, 0.0, pltpu.roll(maps[-1], block, 0))
        after = jnp.where(last_rows, 0.0, pltpu.roll(maps[0], rows - block, 0))
        padded = [before] + maps + [after]
        sums = []
        for q in range(bands):
            down = padded[q] + padded[q + 1] + padded[q + 2]
            left = jnp.where(not_left, pltpu.roll(down, 1, 1), 0.0)
            right = jnp.where(not_right, pltpu.roll(down, LANES - 1, 1), 0.0)
            sums.append(down + left + right)
        return sums

    def swapped(m):
        return jnp.where(even, pltpu.roll(m, rows - 1, 0), pltpu.roll(m, 1, 0))

    def channels(value):
        return [value[c * rows:(c + 1) * rows] for c in range(3)]

    def regrouped(maps):
        turned = {}
        for b, m in enumerate(maps):
            for q in range(bands):
                shift = (b - q) % bands * WIDTH
                if (id(m), shift) not in turned:
                    turned[id(m), shift] = pltpu.roll(m, shift, 1) if shift else m
        out = []
        for q in range(bands):
            parts = [turned[id(m), (b - q) % bands * WIDTH] for b, m in enumerate(maps)]
            value = parts[-1]
            for b in range(bands - 2, -1, -1):
                value = jnp.where(group == b, parts[b], value)
            out.append(value)
        return out

    def self_maps(energy):
        levels = [[weight_var / 27.0 * v + bias_var for v in box(energy)]]
        for _ in range(DEPTH - 1):
            levels.append([weight_var / 18.0 * v + bias_var for v in box(levels[-1])])
        inverse = [[lax.rsqrt(v) for v in level] for level in levels]
        return [[v * r for v, r in zip(*pair)] for pair in zip(levels, inverse)], inverse

    def relu_map(k, scale, inverse, factor):
        u = jnp.maximum(1.0 - jnp.abs(k * inverse), 1e-30)
        u2 = u * u
        root = lax.rsqrt(u)
        a = [factor * v for v in COEFS]
        poly = (a[0] + a[1] * u) + (a[2] + a[3] * u) * u2 + ((a[4] + a[5] * u) + a[6] * u2) * (u2 * u2)
        return (0.5 * factor) * jnp.maximum(k, 0.0) + (scale * u2) * poly * root

    def chosen(flags, first, second):
        first, second = first.reshape(-1, 8, LANES), second.reshape(-1, 8, LANES)
        return jnp.where(flags[None], first, second).reshape(-1, LANES)

    odd = pick_ref[n_tiles] == 1
    cols = [channels(chosen(odd, near_ref[...], passed_ref[...])), channels(far_ref[...])]
    row_values = []
    for s in range(n_tiles):
        value = row_refs[0][...]
        for n, k in enumerate(order, 1):
            value = chosen(pick_ref[s] == k, row_refs[n][...], value)
        row_values.append(channels(value))

    def dot(first, second):
        return sum(a * b for a, b in zip(first, second))

    turned_cols = [[swapped(v) for v in col] for col in cols]
    cross = regrouped([dot(r, c) for s, r in enumerate(row_values) for c in (cols[s], turned_cols[s])])
    row_energy = [dot(r, r) for r in row_values]
    col_energy = [dot(c, c) for c in cols]
    row_std, row_inv = self_maps(regrouped([row_energy[0], row_energy[0], row_energy[1], row_energy[1]]))
    col_maps = regrouped([col_energy[0], col_energy[0], col_energy[1], col_energy[1]])
    col_std, col_inv = self_maps([jnp.where(other_image, swapped(m), m) for m in col_maps])

    levels = [weight_var / 27.0 * v + bias_var for v in box(cross)]
    for l in range(DEPTH):
        last = l == DEPTH - 1
        factor = weight_var / 1024.0 if last else weight_var / 9.0
        mapped = [
            relu_map(k, rs * cs, ri * ci, factor)
            for k, rs, cs, ri, ci in zip(levels, row_std[l], col_std[l], row_inv[l], col_inv[l])
        ]
        if not last:
            levels = [v + bias_var for v in box(mapped)]
    total = sum(mapped)
    total = total[:8] + total[8:]
    total = total + pltpu.roll(total, 4, 0)
    total = total + pltpu.roll(total, 2, 0)
    sub8 = sub[:8]
    a, s, b = sub8 % 2, sub8 // 2 % 2, sub8 // 4
    wanted = 2 * s + jnp.where(a == b, 0, 1)
    value = jnp.sum(jnp.where(group[:8] == wanted, total, 0.0), axis=1, keepdims=True) + bias_var
    value = jnp.broadcast_to(value, (8, LANES))
    result = jnp.where(lane[:8] == 0, value, pltpu.roll(value, 4, 0))
    for s in range(n_tiles):
        out_ref[s] = result[2 * s:2 * s + 2, 0:2]


def local(images, roots):
    n_row, n_col = lax.axis_size("row"), lax.axis_size("col")
    n_tiles = roots.shape[0]
    block, ch, pix = images.shape
    tiles = pix // LANES
    packed = images.reshape(block, ch, tiles, LANES).transpose(1, 2, 0, 3).reshape(ch * tiles * block, LANES)
    powers = n_row & (n_row - 1) == 0
    def moved(value, shift):
        pairs = []
        for i in range(n_row):
            for j in range(n_col):
                row, col = shift(i, j)
                pairs.append((i * n_col + j, row * n_col + col))
        return lax.ppermute(value, ("row", "col"), pairs)

    def row_shift(k, crossed):
        def shift(i, j):
            return (i ^ k if powers else (i + k) % n_row), (j ^ 1 if crossed else j)
        return shift

    near = moved(packed, lambda i, j: (i, j ^ 1))
    far = moved(packed, lambda i, j: (i, (j + 2) % n_col))
    order = [k for k in range(n_row - 1, 0, -1) if k % 2 == 0] + [k for k in range(n_row - 1, 0, -1) if k % 2]
    row_blocks = []
    for k in order:
        crossed = k % 2 == 1
        row_blocks.append(moved(near if crossed else packed, row_shift(k, crossed)))
    passed = moved(far, lambda i, j: (i, j ^ 1))
    vmem = pl.BlockSpec(memory_space=pltpu.VMEM)

    def placed(value):
        return pltpu.with_memory_space_constraint(value, pltpu.VMEM)

    own, pick, near_copy, far_copy = pl.pallas_call(
        lambda *refs: prepare(powers, n_row, *refs),
        out_shape=[pltpu.VMEM(packed.shape, jnp.float32), pltpu.VMEM((n_tiles + 1, 8, LANES), jnp.int32)] + [pltpu.VMEM(packed.shape, jnp.float32)] * 2,
        in_specs=[pl.BlockSpec(memory_space=pltpu.SMEM)] + [vmem] * 3,
        out_specs=[vmem] * 4,
        name="prepare",
    )(roots, packed, placed(near), placed(far))
    return pl.pallas_call(
        lambda *refs: kernel(n_tiles, order, *refs),
        out_shape=jax.ShapeDtypeStruct((n_tiles, block, block), jnp.float32),
        in_specs=[vmem] * (4 + n_row),
        out_specs=vmem,
        name="tiles",
    )(*map(placed, [pick, near_copy, far_copy, passed, own, *row_blocks]))


def solution(mesh):
    in_specs = (P(("row", "col"), None, None), P())
    out_specs = P(None, "row", "col")
    return jax.shard_map(local, mesh=mesh, in_specs=in_specs, out_specs=out_specs, check_vma=False)
```

time: 10.5 us -> 10.3 us (0.981)
  Pallas kernels: 2.79 us -> 2 us
  waiting for transfers between devices: 1.23 us -> 1.81 us
    ppermute x6, waiting for transfers between devices: 1.23 us -> 1.81 us  [moved(): return lax.ppermute(value, ('row', 'col'), pairs)]
    pallas_call x1, Pallas kernels: 1.34 us -> 0.76 us  [local(): pl.pallas_call(lambda *refs: prepare(powers, n_row, *refs), out_shape=[pl...]
    pallas_call x1, Pallas kernels: 1.46 us -> 1.24 us  [local(): pl.pallas_call(lambda *refs: kernel(n_tiles, order, *refs), out_shape=jax...]
  transfers between devices with their start and end apart: 6 -> 6, of which waited for: 2 -> 3; matrix products, arithmetic and copies ran while one was open for 0% -> 0% of each run, Pallas kernels for 13% -> 8%
where the time goes in v5:
time: 10.3 us; the launch traced here: 10.1 us
  starting transfers between devices  6.31 us (61%)
  Pallas kernels  2 us (19%)
  waiting for transfers between devices  1.81 us (18%)
    ppermute x6, starting transfers between devices, moved(): return lax.ppermute(value, ('row', 'col'), pairs)  6.31 us
    ppermute x6, waiting for transfers between devices, moved(): return lax.ppermute(value, ('row', 'col'), pairs)  1.81 us
    pallas_call x1, Pallas kernels, local(): pl.pallas_call(lambda *refs: kernel(n_tiles, order, *refs), out_shape=jax...  1.24 us
    pallas_call x1, Pallas kernels, local(): pl.pallas_call(lambda *refs: prepare(powers, n_row, *refs), out_shape=[pl...  0.76 us
  transfers between devices with their start and end apart: 6, of which 3 were waited for; matrix products, arithmetic and copies ran while one was open for 0% of the time, Pallas kernels for 8%

profile of v5, /device:TPU:1, one launch (start us, length us, event | category | flops | bytes accessed | tf_op | source)
XLA Modules:
  0.0 10.1 jit_solution(2748555700088678150)
XLA Ops:
  0.0 0.1 collective-permute-start
  0.1 2.7 %collective-permute-start.1 = (f32[48,128]{1,0:T(8,128)}, f32[48,128]{1,0:T(8,128)S(1)}, u32[]{:S(2)}, u32[]{:S(2)}) collective-permute-start(f32[48,128]{1,0:T(8,128)} %bitcast.6), channel_id=1, source_target_pairs={{0,2},{1,3},{2,4},{3,5},{4,6},{5,7},{6,0},{7,1},{8,10},{9,11},{10,... | collective-permute-start | bytes 73736 | tf_op jit(solution)/shard_map/ppermute | solution.py:170
  2.8 1.2 %collective-permute-start.3 = (f32[48,128]{1,0:T(8,128)}, f32[48,128]{1,0:T(8,128)S(1)}, u32[]{:S(2)}, u32[]{:S(2)}) collective-permute-start(f32[48,128]{1,0:T(8,128)} %bitcast.7), channel_id=1, source_target_pairs={{0,16},{1,17},{2,18},{3,19},{4,20},{5,21},{6,22},{7,23},{8,24},{9,... | collective-permute-start | bytes 73736 | tf_op jit(solution)/shard_map/ppermute | solution.py:170
  4.0 0.0 collective-permute-done.refs_2_
  4.0 1.6 %collective-permute-start.4 = (f32[48,128]{1,0:T(8,128)S(1)}, f32[48,128]{1,0:T(8,128)S(1)}, u32[]{:S(2)}, u32[]{:S(2)}) collective-permute-start(f32[48,128]{1,0:T(8,128)S(1)} %collective-permute-done.refs_2_), channel_id=1, source_target_pairs={{0,25},{1,24},{2,27},{3,26},{4,29},{5,28},{6,31},{7,30},{8,17},{9,... | collective-permute-start | bytes 73736 | tf_op jit(solution)/shard_map/ppermute | solution.py:170
  5.6 0.1 collective-permute-start.5
  5.7 0.9 %collective-permute-done.1.refs_3_ = f32[48,128]{1,0:T(8,128)S(1)} collective-permute-done((f32[48,128]{1,0:T(8,128)}, f32[48,128]{1,0:T(8,128)S(1)}, u32[]{:S(2)}, u32[]{:S(2)}) %collective-permute-start.1) | collective-permute-done | bytes 24608 | tf_op jit(solution)/shard_map/ppermute | solution.py:170
  6.6 0.6 %collective-permute-start.2 = (f32[48,128]{1,0:T(8,128)S(1)}, f32[48,128]{1,0:T(8,128)S(1)}, u32[]{:S(2)}, u32[]{:S(2)}) collective-permute-start(f32[48,128]{1,0:T(8,128)S(1)} %collective-permute-done.1.refs_3_), channel_id=1, source_target_pairs={{0,1},{1,0},{2,3},{3,2},{4,5},{5,4},{6,7},{7,6},{8,9},{9,8},{10,11... | collective-permute-start | bytes 73736 | tf_op jit(solution)/shard_map/ppermute | solution.py:170
  7.2 0.8 %prepare.1 = (f32[48,128]{1,0:T(8,128)S(1)}, s32[3,8,128]{2,1,0:T(8,128)S(1)}, f32[48,128]{1,0:T(8,128)S(1)}, f32[48,128]{1,0:T(8,128)S(1)}) custom-call(s32[2,8]{1,0:T(2,128)} %refs_0_.1, f32[48,128]{1,0:T(8,128)} %bitcast.8, f32[48,128]{1,0:T(8,128)S(1)} %collective-permute-done.refs_2_, f32[48,128]{1,0:T(8,128)S(1)} %collective-permute-done.1.refs_3_), custom_call_target="tpu_custom_call" | custom-call | tf_op jit(solution)/shard_map/prepare/pallas_call | solution.py:190
  8.0 0.0 collective-permute-done.3.refs_5_
  8.0 0.5 %collective-permute-done.4.refs_6_ = f32[48,128]{1,0:T(8,128)S(1)} collective-permute-done((f32[48,128]{1,0:T(8,128)S(1)}, f32[48,128]{1,0:T(8,128)S(1)}, u32[]{:S(2)}, u32[]{:S(2)}) %collective-permute-start.4) | collective-permute-done | bytes 24608 | tf_op jit(solution)/shard_map/ppermute | solution.py:170
  8.5 0.4 %collective-permute-done.5.refs_7_ = f32[48,128]{1,0:T(8,128)S(1)} collective-permute-done((f32[48,128]{1,0:T(8,128)S(1)}, f32[48,128]{1,0:T(8,128)S(1)}, u32[]{:S(2)}, u32[]{:S(2)}) %collective-permute-start.5) | collective-permute-done | bytes 24608 | tf_op jit(solution)/shard_map/ppermute | solution.py:170
  8.9 0.0 collective-permute-done.2.refs_3_
  8.9 1.2 %tiles.1 = f32[2,2,2]{2,1,0:T(2,128)} custom-call(s32[3,8,128]{2,1,0:T(8,128)S(1)} %get-tuple-element.9.refs_0_, f32[48,128]{1,0:T(8,128)S(1)} %get-tuple-element.10.refs_1_, f32[48,128]{1,0:T(8,128)S(1)} %get-tuple-element.11.refs_2_, f32[48,128]{1,0:T(8,128)S(1)} %collective-permute-done.2.refs_3_, f32[48,128]{1,0:T(8,128)S(1)} %get-tuple-element.12.refs_4_, ...), custom_call_target="tpu_custom_call" | custom-call | tf_op jit(solution)/shard_map/tiles/pallas_call | solution.py:197
Async XLA Ops:
  0.0 4.0 %collective-permute-start = (f32[48,128]{1,0:T(8,128)}, f32[48,128]{1,0:T(8,128)S(1)}, u32[]{:S(2)}, u32[]{:S(2)}) collective-permute-start(f32[48,128]{1,0:T(8,128)} %bitcast.5), channel_id=1, source_target_pairs={{0,1},{1,0},{2,3},{3,2},{4,5},{5,4},{6,7},{7,6},{8,9},{9,8},{10,11... | collective-permute-start | bytes 73736 | tf_op jit(solution)/shard_map/ppermute | solution.py:170
  0.1 6.6 %collective-permute-start.1 = (f32[48,128]{1,0:T(8,128)}, f32[48,128]{1,0:T(8,128)S(1)}, u32[]{:S(2)}, u32[]{:S(2)}) collective-permute-start(f32[48,128]{1,0:T(8,128)} %bitcast.6), channel_id=1, source_target_pairs={{0,2},{1,3},{2,4},{3,5},{4,6},{5,7},{6,0},{7,1},{8,10},{9,11},{10,... | collective-permute-start | bytes 73736 | tf_op jit(solution)/shard_map/ppermute | solution.py:170
  2.8 5.2 %collective-permute-start.3 = (f32[48,128]{1,0:T(8,128)}, f32[48,128]{1,0:T(8,128)S(1)}, u32[]{:S(2)}, u32[]{:S(2)}) collective-permute-start(f32[48,128]{1,0:T(8,128)} %bitcast.7), channel_id=1, source_target_pairs={{0,16},{1,17},{2,18},{3,19},{4,20},{5,21},{6,22},{7,23},{8,24},{9,... | collective-permute-start | bytes 73736 | tf_op jit(solution)/shard_map/ppermute | solution.py:170
  4.0 4.5 %collective-permute-start.4 = (f32[48,128]{1,0:T(8,128)S(1)}, f32[48,128]{1,0:T(8,128)S(1)}, u32[]{:S(2)}, u32[]{:S(2)}) collective-permute-start(f32[48,128]{1,0:T(8,128)S(1)} %collective-permute-done.refs_2_), channel_id=1, source_target_pairs={{0,25},{1,24},{2,27},{3,26},{4,29},{5,28},{6,31},{7,30},{8,17},{9,... | collective-permute-start | bytes 73736 | tf_op jit(solution)/shard_map/ppermute | solution.py:170
  5.6 3.3 %collective-permute-start.5 = (f32[48,128]{1,0:T(8,128)S(1)}, f32[48,128]{1,0:T(8,128)S(1)}, u32[]{:S(2)}, u32[]{:S(2)}) collective-permute-start(f32[48,128]{1,0:T(8,128)S(1)} %collective-permute-done.refs_2_), channel_id=1, source_target_pairs={{0,9},{1,8},{2,11},{3,10},{4,13},{5,12},{6,15},{7,14},{8,1},{9,0},... | collective-permute-start | bytes 73736 | tf_op jit(solution)/shard_map/ppermute | solution.py:170
  6.6 2.3 %collective-permute-start.2 = (f32[48,128]{1,0:T(8,128)S(1)}, f32[48,128]{1,0:T(8,128)S(1)}, u32[]{:S(2)}, u32[]{:S(2)}) collective-permute-start(f32[48,128]{1,0:T(8,128)S(1)} %collective-permute-done.1.refs_3_), channel_id=1, source_target_pairs={{0,1},{1,0},{2,3},{3,2},{4,5},{5,4},{6,7},{7,6},{8,9},{9,8},{10,11... | collective-permute-start | bytes 73736 | tf_op jit(solution)/shard_map/ppermute | solution.py:170

commit v6 on v5

--- a/solution.py
+++ b/solution.py
@@ -32,22 +32,41 @@
 COEFS = [float(v) / (2.0 * math.pi) for v in remainder_coefficients()]
 
 
-def prepare(powers, n_row, roots_ref, own_ref, near_ref, far_ref, own_out, pick_out, near_out, far_out):
+def join(own_ref, near_ref, tile_ref, both_out):
+    rows = own_ref.shape[0]
+    both_out[pl.ds(0, rows)] = own_ref[...]
+    both_out[pl.ds(rows, rows)] = near_ref[...]
+
+
+def blank(out):
+    out[...] = jnp.zeros(out.shape, out.dtype)
+
+
+def relay(near_ref, near_out):
+    near_out[...] = near_ref[...]
+
+
+def first_half(both_ref, half_out):
+    half_out[...] = both_ref[pl.ds(0, half_out.shape[0])]
+
+
+def prepare(row_source, slots, roots_ref, far_ref, pick_out, far_out):
     n_tiles = roots_ref.shape[0]
     row_index, col_index = lax.axis_index("row"), lax.axis_index("col")
-    own_out[...] = own_ref[...]
-    near_out[...] = near_ref[...]
+    odd = lax.rem(col_index, 2)
     far_out[...] = far_ref[...]
     for s in range(n_tiles):
-        root = roots_ref[s, col_index]
-        source = root ^ row_index if powers else lax.rem(row_index - root + n_row, n_row)
-        pick_out[s] = jnp.full((8, LANES), source, jnp.int32)
-    pick_out[n_tiles] = jnp.full((8, LANES), lax.rem(col_index, 2), jnp.int32)
-
-
-def kernel(n_tiles, order, pick_ref, near_ref, far_ref, passed_ref, *refs):
+        source = row_source(row_index, roots_ref[s, col_index])
+        slot = jnp.int32(0)
+        for n, (on_even, on_odd) in enumerate(slots, 1):
+            slot = jnp.where(source == jnp.where(odd == 1, on_odd, on_even), n, slot)
+        pick_out[s] = jnp.full((8, LANES), slot, jnp.int32)
+    pick_out[n_tiles] = jnp.full((8, LANES), odd, jnp.int32)
+
+
+def kernel(n_tiles, pick_ref, far_ref, passed_ref, both_ref, *refs):
     row_refs, out_ref = refs[:-1], refs[-1]
-    block = row_refs[0].shape[0] // 24
+    block = far_ref.shape[0] // 24
     rows, bands = 8 * block, LANES // WIDTH
     sub = lax.broadcasted_iota(jnp.int32, (rows, LANES), 0)
     lane = lax.broadcasted_iota(jnp.int32, (rows, LANES), 1)
@@ -111,12 +130,12 @@
         return jnp.where(flags[None], first, second).reshape(-1, LANES)
 
     odd = pick_ref[n_tiles] == 1
-    cols = [channels(chosen(odd, near_ref[...], passed_ref[...])), channels(far_ref[...])]
+    cols = [channels(chosen(odd, both_ref[pl.ds(3 * rows, 3 * rows)], passed_ref[...])), channels(far_ref[...])]
     row_values = []
     for s in range(n_tiles):
-        value = row_refs[0][...]
-        for n, k in enumerate(order, 1):
-            value = chosen(pick_ref[s] == k, row_refs[n][...], value)
+        value = both_ref[pl.ds(0, 3 * rows)]
+        for n, ref in enumerate(row_refs, 1):
+            value = chosen(pick_ref[s] == n, ref[pl.ds(ref.shape[0] - 3 * rows, 3 * rows)], value)
         row_values.append(channels(value))
 
     def dot(first, second):
@@ -161,46 +180,63 @@
     tiles = pix // LANES
     packed = images.reshape(block, ch, tiles, LANES).transpose(1, 2, 0, 3).reshape(ch * tiles * block, LANES)
     powers = n_row & (n_row - 1) == 0
-    def moved(value, shift):
+
+    def row_target(i, k):
+        return i ^ k if powers else (i + k) % n_row
+
+    def row_source(row_index, root):
+        return root ^ row_index if powers else lax.rem(row_index - root + n_row, n_row)
+
+    def moved(value, target):
         pairs = []
         for i in range(n_row):
             for j in range(n_col):
-                row, col = shift(i, j)
+                row, col = target(i, j)
                 pairs.append((i * n_col + j, row * n_col + col))
         return lax.ppermute(value, ("row", "col"), pairs)
 
-    def row_shift(k, crossed):
-        def shift(i, j):
-            return (i ^ k if powers else (i + k) % n_row), (j ^ 1 if crossed else j)
-        return shift
-
-    near = moved(packed, lambda i, j: (i, j ^ 1))
-    far = moved(packed, lambda i, j: (i, (j + 2) % n_col))
-    order = [k for k in range(n_row - 1, 0, -1) if k % 2 == 0] + [k for k in range(n_row - 1, 0, -1) if k % 2]
-    row_blocks = []
-    for k in order:
-        crossed = k % 2 == 1
-        row_blocks.append(moved(near if crossed else packed, row_shift(k, crossed)))
-    passed = moved(far, lambda i, j: (i, j ^ 1))
-    vmem = pl.BlockSpec(memory_space=pltpu.VMEM)
-
     def placed(value):
         return pltpu.with_memory_space_constraint(value, pltpu.VMEM)
 
-    own, pick, near_copy, far_copy = pl.pallas_call(
-        lambda *refs: prepare(powers, n_row, *refs),
-        out_shape=[pltpu.VMEM(packed.shape, jnp.float32), pltpu.VMEM((n_tiles + 1, 8, LANES), jnp.int32)] + [pltpu.VMEM(packed.shape, jnp.float32)] * 2,
-        in_specs=[pl.BlockSpec(memory_space=pltpu.SMEM)] + [vmem] * 3,
-        out_specs=[vmem] * 4,
+    vmem = pl.BlockSpec(memory_space=pltpu.VMEM)
+    single = pltpu.VMEM(packed.shape, jnp.float32)
+    double = pltpu.VMEM((2 * packed.shape[0], LANES), jnp.float32)
+
+    def on_core(body, out_shape, *values, flops=0):
+        return pl.pallas_call(
+            body, out_shape=out_shape, in_specs=[vmem] * len(values), out_specs=vmem, name=body.__name__,
+            cost_estimate=pl.CostEstimate(flops=flops, bytes_accessed=0, transcendentals=0),
+        )(*map(placed, values))
+
+    near = moved(packed, lambda i, j: (i, j ^ 1))
+    tile = on_core(blank, pltpu.VMEM((8, LANES), jnp.float32), flops=3000000)
+    ahead, tile = lax.optimization_barrier((packed, tile))
+    far = moved(ahead, lambda i, j: (i, (j + 2) % n_col))
+    both = on_core(join, double, packed, on_core(relay, single, near, flops=3000000), tile)
+    row_blocks, slots = [], []
+    for k in range(1, n_row - 1, 2):
+        pair = moved(both, lambda i, j, k=k: (row_target(i, k + 1 if j % 2 == 0 else k), j ^ 1))
+        swapped = moved(on_core(first_half, single, pair), lambda i, j: (i, j ^ 1))
+        row_blocks += [pair, swapped]
+        slots += [(k, k + 1), (k + 1, k)]
+    if n_row % 2 == 0:
+        row_blocks.append(moved(on_core(relay, single, near, flops=20_000_000_000), lambda i, j: (row_target(i, n_row - 1), j ^ 1)))
+        slots.append((n_row - 1, n_row - 1))
+    passed = moved(far, lambda i, j: (i, j ^ 1))
+    pick, far_copy = pl.pallas_call(
+        lambda *refs: prepare(row_source, slots, *refs),
+        out_shape=[pltpu.VMEM((n_tiles + 1, 8, LANES), jnp.int32), single],
+        in_specs=[pl.BlockSpec(memory_space=pltpu.SMEM), vmem],
+        out_specs=[vmem] * 2,
         name="prepare",
-    )(roots, packed, placed(near), placed(far))
+    )(roots, placed(far))
     return pl.pallas_call(
-        lambda *refs: kernel(n_tiles, order, *refs),
+        lambda *refs: kernel(n_tiles, *refs),
         out_shape=jax.ShapeDtypeStruct((n_tiles, block, block), jnp.float32),
-        in_specs=[vmem] * (4 + n_row),
+        in_specs=[vmem] * (4 + len(row_blocks)),
         out_specs=vmem,
         name="tiles",
-    )(*map(placed, [pick, near_copy, far_copy, passed, own, *row_blocks]))
+    )(*map(placed, [pick, far_copy, passed, both, *row_blocks]))
 
 
 def solution(mesh):

time: 10.3 us -> 10 us (0.971)
  the two profiles are of different devices: /device:TPU:1 before, /device:TPU:0 now
where the time goes in v6:
time: 10 us; the launch traced here: 9.86 us
  starting transfers between devices  6.35 us (64%)
  Pallas kernels  1.96 us (20%)
  waiting for transfers between devices  1.51 us (15%)
    ppermute x6, starting transfers between devices, moved(): return lax.ppermute(value, ('row', 'col'), pairs)  6.35 us
    ppermute x6, waiting for transfers between devices, moved(): return lax.ppermute(value, ('row', 'col'), pairs)  1.51 us
    pallas_call x1, Pallas kernels, local(): pl.pallas_call(lambda *refs: kernel(n_tiles, *refs), out_shape=jax.ShapeD...  1.24 us
    pallas_call x1, Pallas kernels, local(): pl.pallas_call(lambda *refs: prepare(row_source, slots, *refs), out_shape...  0.71 us
  transfers between devices with their start and end apart: 6, of which 2 were waited for; matrix products, arithmetic and copies ran while one was open for 0% of the time, Pallas kernels for 7%

profile of v6, /device:TPU:0, one launch (start us, length us, event | category | flops | bytes accessed | tf_op | source)
XLA Modules:
  0.0 9.9 jit_solution(2996216871110487804)
XLA Ops:
  0.0 0.5 %collective-permute-start.2 = (f32[48,128]{1,0:T(8,128)}, f32[48,128]{1,0:T(8,128)S(1)}, u32[]{:S(2)}, u32[]{:S(2)}) collective-permute-start(f32[48,128]{1,0:T(8,128)} %bitcast.5), channel_id=1, source_target_pairs={{0,1},{1,0},{2,3},{3,2},{4,5},{5,4},{6,7},{7,6},{8,9},{9,8},{10,11... | collective-permute-start | bytes 73736 | tf_op jit(solution)/shard_map/ppermute | solution.py:196
  0.5 0.0 copy-start
  0.5 2.6 %collective-permute-start = (f32[48,128]{1,0:T(8,128)}, f32[48,128]{1,0:T(8,128)S(1)}, u32[]{:S(2)}, u32[]{:S(2)}) collective-permute-start(f32[48,128]{1,0:T(8,128)} %bitcast.6), channel_id=1, source_target_pairs={{0,2},{1,3},{2,4},{3,5},{4,6},{5,7},{6,0},{7,1},{8,10},{9,11},{10,... | collective-permute-start | bytes 73736 | tf_op jit(solution)/shard_map/ppermute | solution.py:196
  3.1 0.0 collective-permute-done.2.near_ref
  3.1 0.0 copy-done
  3.1 1.3 %collective-permute-start.3 = (f32[96,128]{1,0:T(8,128)S(1)}, f32[96,128]{1,0:T(8,128)S(1)}, u32[]{:S(2)}, u32[]{:S(2)}) collective-permute-start(f32[96,128]{1,0:T(8,128)S(1)} %join.1.refs_3_), channel_id=1, source_target_pairs={{0,17},{1,8},{2,19},{3,10},{4,21},{5,12},{6,23},{7,14},{8,25},{9,0... | collective-permute-start | bytes 147464 | tf_op jit(solution)/shard_map/ppermute | solution.py:196
  4.5 1.4 %collective-permute-start.5 = (f32[48,128]{1,0:T(8,128)S(1)}, f32[48,128]{1,0:T(8,128)S(1)}, u32[]{:S(2)}, u32[]{:S(2)}) collective-permute-start(f32[48,128]{1,0:T(8,128)S(1)} %relay.3), channel_id=1, source_target_pairs={{0,25},{1,24},{2,27},{3,26},{4,29},{5,28},{6,31},{7,30},{8,17},{9,... | collective-permute-start | bytes 73736 | tf_op jit(solution)/shard_map/ppermute | solution.py:196
  5.9 1.3 %collective-permute-done.refs_1_ = f32[48,128]{1,0:T(8,128)S(1)} collective-permute-done((f32[48,128]{1,0:T(8,128)}, f32[48,128]{1,0:T(8,128)S(1)}, u32[]{:S(2)}, u32[]{:S(2)}) %collective-permute-start) | collective-permute-done | bytes 24608 | tf_op jit(solution)/shard_map/ppermute | solution.py:196
  7.2 0.0 collective-permute-start.1
  7.2 0.0 collective-permute-done.3.both_ref.refs_4_
  7.2 0.5 %collective-permute-start.4 = (f32[48,128]{1,0:T(8,128)S(1)}, f32[48,128]{1,0:T(8,128)S(1)}, u32[]{:S(2)}, u32[]{:S(2)}) collective-permute-start(f32[48,128]{1,0:T(8,128)S(1)} %first_half.1), channel_id=1, source_target_pairs={{0,1},{1,0},{2,3},{3,2},{4,5},{5,4},{6,7},{7,6},{8,9},{9,8},{10,11... | collective-permute-start | bytes 73736 | tf_op jit(solution)/shard_map/ppermute | solution.py:196
  7.7 0.7 %prepare.1 = (s32[3,8,128]{2,1,0:T(8,128)S(1)}, f32[48,128]{1,0:T(8,128)S(1)}) custom-call(s32[2,8]{1,0:T(2,128)} %refs_0_.1, f32[48,128]{1,0:T(8,128)S(1)} %collective-permute-done.refs_1_), custom_call_target="tpu_custom_call" | custom-call | tf_op jit(solution)/shard_map/prepare/pallas_call | solution.py:226
  8.5 0.0 collective-permute-done.1.refs_2_
  8.5 0.2 %collective-permute-done.5.refs_6_ = f32[48,128]{1,0:T(8,128)S(1)} collective-permute-done((f32[48,128]{1,0:T(8,128)S(1)}, f32[48,128]{1,0:T(8,128)S(1)}, u32[]{:S(2)}, u32[]{:S(2)}) %collective-permute-start.5) | collective-permute-done | bytes 24608 | tf_op jit(solution)/shard_map/ppermute | solution.py:196
  8.6 0.0 collective-permute-done.4.refs_5_
  8.6 1.2 %tiles.1 = f32[2,2,2]{2,1,0:T(2,128)} custom-call(s32[3,8,128]{2,1,0:T(8,128)S(1)} %get-tuple-element.10.refs_0_, f32[48,128]{1,0:T(8,128)S(1)} %get-tuple-element.11.refs_1_, f32[48,128]{1,0:T(8,128)S(1)} %collective-permute-done.1.refs_2_, f32[96,128]{1,0:T(8,128)S(1)} %join.1.refs_3_, f32[96,128]{1,0:T(8,128)S(1)} %collective-permute-done.3.both_ref.refs_4_, ...), custom_call_target="tpu_custom_call" | custom-call | tf_op jit(solution)/shard_map/tiles/pallas_call | solution.py:233
  (5 shorter events, 0.0 us)
Async XLA Ops:
  0.0 3.1 %collective-permute-start.2 = (f32[48,128]{1,0:T(8,128)}, f32[48,128]{1,0:T(8,128)S(1)}, u32[]{:S(2)}, u32[]{:S(2)}) collective-permute-start(f32[48,128]{1,0:T(8,128)} %bitcast.5), channel_id=1, source_target_pairs={{0,1},{1,0},{2,3},{3,2},{4,5},{5,4},{6,7},{7,6},{8,9},{9,8},{10,11... | collective-permute-start | bytes 73736 | tf_op jit(solution)/shard_map/ppermute | solution.py:196
  0.5 2.6 %copy-start = (f32[2,3,1024]{2,0,1:T(2,128)S(1)}, f32[2,3,1024]{2,0,1:T(2,128)}, u32[]{:S(2)}) copy-start(f32[2,3,1024]{2,0,1:T(2,128)} %param.2) | copy-start | bytes 73732
  0.5 6.8 %collective-permute-start = (f32[48,128]{1,0:T(8,128)}, f32[48,128]{1,0:T(8,128)S(1)}, u32[]{:S(2)}, u32[]{:S(2)}) collective-permute-start(f32[48,128]{1,0:T(8,128)} %bitcast.6), channel_id=1, source_target_pairs={{0,2},{1,3},{2,4},{3,5},{4,6},{5,7},{6,0},{7,1},{8,10},{9,11},{10,... | collective-permute-start | bytes 73736 | tf_op jit(solution)/shard_map/ppermute | solution.py:196
  3.1 4.1 %collective-permute-start.3 = (f32[96,128]{1,0:T(8,128)S(1)}, f32[96,128]{1,0:T(8,128)S(1)}, u32[]{:S(2)}, u32[]{:S(2)}) collective-permute-start(f32[96,128]{1,0:T(8,128)S(1)} %join.1.refs_3_), channel_id=1, source_target_pairs={{0,17},{1,8},{2,19},{3,10},{4,21},{5,12},{6,23},{7,14},{8,25},{9,0... | collective-permute-start | bytes 147464 | tf_op jit(solution)/shard_map/ppermute | solution.py:196
  4.5 4.2 %collective-permute-start.5 = (f32[48,128]{1,0:T(8,128)S(1)}, f32[48,128]{1,0:T(8,128)S(1)}, u32[]{:S(2)}, u32[]{:S(2)}) collective-permute-start(f32[48,128]{1,0:T(8,128)S(1)} %relay.3), channel_id=1, source_target_pairs={{0,25},{1,24},{2,27},{3,26},{4,29},{5,28},{6,31},{7,30},{8,17},{9,... | collective-permute-start | bytes 73736 | tf_op jit(solution)/shard_map/ppermute | solution.py:196
  7.2 1.2 %collective-permute-start.1 = (f32[48,128]{1,0:T(8,128)S(1)}, f32[48,128]{1,0:T(8,128)S(1)}, u32[]{:S(2)}, u32[]{:S(2)}) collective-permute-start(f32[48,128]{1,0:T(8,128)S(1)} %collective-permute-done.refs_1_), channel_id=1, source_target_pairs={{0,1},{1,0},{2,3},{3,2},{4,5},{5,4},{6,7},{7,6},{8,9},{9,8},{10,11... | collective-permute-start | bytes 73736 | tf_op jit(solution)/shard_map/ppermute | solution.py:196
  7.2 1.4 %collective-permute-start.4 = (f32[48,128]{1,0:T(8,128)S(1)}, f32[48,128]{1,0:T(8,128)S(1)}, u32[]{:S(2)}, u32[]{:S(2)}) collective-permute-start(f32[48,128]{1,0:T(8,128)S(1)} %first_half.1), channel_id=1, source_target_pairs={{0,1},{1,0},{2,3},{3,2},{4,5},{5,4},{6,7},{7,6},{8,9},{9,8},{10,11... | collective-permute-start | bytes 73736 | tf_op jit(solution)/shard_map/ppermute | solution.py:196

commit v7 on v6

--- a/solution.py
+++ b/solution.py
@@ -50,11 +50,10 @@
     half_out[...] = both_ref[pl.ds(0, half_out.shape[0])]
 
 
-def prepare(row_source, slots, roots_ref, far_ref, pick_out, far_out):
+def prepare(row_source, slots, roots_ref, pick_out):
     n_tiles = roots_ref.shape[0]
     row_index, col_index = lax.axis_index("row"), lax.axis_index("col")
     odd = lax.rem(col_index, 2)
-    far_out[...] = far_ref[...]
     for s in range(n_tiles):
         source = row_source(row_index, roots_ref[s, col_index])
         slot = jnp.int32(0)
@@ -130,7 +129,7 @@
         return jnp.where(flags[None], first, second).reshape(-1, LANES)
 
     odd = pick_ref[n_tiles] == 1
-    cols = [channels(chosen(odd, both_ref[pl.ds(3 * rows, 3 * rows)], passed_ref[...])), channels(far_ref[...])]
+    cols = [channels(chosen(odd, both_ref[pl.ds(3 * rows, 3 * rows)], far_ref[...])), channels(passed_ref[...])]
     row_values = []
     for s in range(n_tiles):
         value = both_ref[pl.ds(0, 3 * rows)]
@@ -211,7 +210,7 @@
     near = moved(packed, lambda i, j: (i, j ^ 1))
     tile = on_core(blank, pltpu.VMEM((8, LANES), jnp.float32), flops=3000000)
     ahead, tile = lax.optimization_barrier((packed, tile))
-    far = moved(ahead, lambda i, j: (i, (j + 2) % n_col))
+    far = moved(ahead, lambda i, j: (i, ((j + 2) % n_col) ^ 1))
     both = on_core(join, double, packed, on_core(relay, single, near, flops=3000000), tile)
     row_blocks, slots = [], []
     for k in range(1, n_row - 1, 2):
@@ -223,20 +222,20 @@
         row_blocks.append(moved(on_core(relay, single, near, flops=20_000_000_000), lambda i, j: (row_target(i, n_row - 1), j ^ 1)))
         slots.append((n_row - 1, n_row - 1))
     passed = moved(far, lambda i, j: (i, j ^ 1))
-    pick, far_copy = pl.pallas_call(
+    pick = pl.pallas_call(
         lambda *refs: prepare(row_source, slots, *refs),
-        out_shape=[pltpu.VMEM((n_tiles + 1, 8, LANES), jnp.int32), single],
-        in_specs=[pl.BlockSpec(memory_space=pltpu.SMEM), vmem],
-        out_specs=[vmem] * 2,
+        out_shape=pltpu.VMEM((n_tiles + 1, 8, LANES), jnp.int32),
+        in_specs=[pl.BlockSpec(memory_space=pltpu.SMEM)],
+        out_specs=vmem,
         name="prepare",
-    )(roots, placed(far))
+    )(roots)
     return pl.pallas_call(
         lambda *refs: kernel(n_tiles, *refs),
         out_shape=jax.ShapeDtypeStruct((n_tiles, block, block), jnp.float32),
         in_specs=[vmem] * (4 + len(row_blocks)),
         out_specs=vmem,
         name="tiles",
-    )(*map(placed, [pick, far_copy, passed, both, *row_blocks]))
+    )(*map(placed, [pick, far, passed, both, *row_blocks]))
 
 
 def solution(mesh):

time: 10 us -> 9.97 us (level)
  waiting for transfers between devices: 1.51 us -> 1.4 us
    ppermute x6, waiting for transfers between devices: 1.51 us -> 1.4 us  [moved(): return lax.ppermute(value, ('row', 'col'), pairs)]
where the time goes in v7:
time: 9.97 us; the launch traced here: 9.81 us
  starting transfers between devices  6.4 us (64%)
  Pallas kernels  1.96 us (20%)
  waiting for transfers between devices  1.4 us (14%)
    ppermute x6, starting transfers between devices, moved(): return lax.ppermute(value, ('row', 'col'), pairs)  6.4 us
    ppermute x6, waiting for transfers between devices, moved(): return lax.ppermute(value, ('row', 'col'), pairs)  1.4 us
    pallas_call x1, Pallas kernels, local(): pl.pallas_call(lambda *refs: kernel(n_tiles, *refs), out_shape=jax.ShapeD...  1.24 us
    pallas_call x1, Pallas kernels, local(): pl.pallas_call(lambda *refs: prepare(row_source, slots, *refs), out_shape...  0.71 us
  transfers between devices with their start and end apart: 6, of which 2 were waited for; matrix products, arithmetic and copies ran while one was open for 0% of the time, Pallas kernels for 7%

profile of v7, /device:TPU:0, one launch (start us, length us, event | category | flops | bytes accessed | tf_op | source)
XLA Modules:
  0.0 9.8 jit_solution(10689894778889151646)
XLA Ops:
  0.0 0.5 %collective-permute-start.2 = (f32[48,128]{1,0:T(8,128)}, f32[48,128]{1,0:T(8,128)S(1)}, u32[]{:S(2)}, u32[]{:S(2)}) collective-permute-start(f32[48,128]{1,0:T(8,128)} %bitcast.5), channel_id=1, source_target_pairs={{0,1},{1,0},{2,3},{3,2},{4,5},{5,4},{6,7},{7,6},{8,9},{9,8},{10,11... | collective-permute-start | bytes 73736 | tf_op jit(solution)/shard_map/ppermute | solution.py:195
  0.5 0.0 copy-start
  0.5 2.7 %collective-permute-start = (f32[48,128]{1,0:T(8,128)}, f32[48,128]{1,0:T(8,128)S(1)}, u32[]{:S(2)}, u32[]{:S(2)}) collective-permute-start(f32[48,128]{1,0:T(8,128)} %bitcast.6), channel_id=1, source_target_pairs={{0,3},{1,2},{2,5},{3,4},{4,7},{5,6},{6,1},{7,0},{8,11},{9,10},{10,... | collective-permute-start | bytes 73736 | tf_op jit(solution)/shard_map/ppermute | solution.py:195
  3.1 0.0 collective-permute-done.2.near_ref
  3.2 0.0 copy-done
  3.2 1.2 %collective-permute-start.3 = (f32[96,128]{1,0:T(8,128)S(1)}, f32[96,128]{1,0:T(8,128)S(1)}, u32[]{:S(2)}, u32[]{:S(2)}) collective-permute-start(f32[96,128]{1,0:T(8,128)S(1)} %join.1.refs_3_), channel_id=1, source_target_pairs={{0,17},{1,8},{2,19},{3,10},{4,21},{5,12},{6,23},{7,14},{8,25},{9,0... | collective-permute-start | bytes 147464 | tf_op jit(solution)/shard_map/ppermute | solution.py:195
  4.4 1.5 %collective-permute-start.5 = (f32[48,128]{1,0:T(8,128)S(1)}, f32[48,128]{1,0:T(8,128)S(1)}, u32[]{:S(2)}, u32[]{:S(2)}) collective-permute-start(f32[48,128]{1,0:T(8,128)S(1)} %relay.3), channel_id=1, source_target_pairs={{0,25},{1,24},{2,27},{3,26},{4,29},{5,28},{6,31},{7,30},{8,17},{9,... | collective-permute-start | bytes 73736 | tf_op jit(solution)/shard_map/ppermute | solution.py:195
  5.9 1.1 %collective-permute-done.refs_1_ = f32[48,128]{1,0:T(8,128)S(1)} collective-permute-done((f32[48,128]{1,0:T(8,128)}, f32[48,128]{1,0:T(8,128)S(1)}, u32[]{:S(2)}, u32[]{:S(2)}) %collective-permute-start) | collective-permute-done | bytes 24608 | tf_op jit(solution)/shard_map/ppermute | solution.py:195
  7.0 0.1 %collective-permute-start.1 = (f32[48,128]{1,0:T(8,128)S(1)}, f32[48,128]{1,0:T(8,128)S(1)}, u32[]{:S(2)}, u32[]{:S(2)}) collective-permute-start(f32[48,128]{1,0:T(8,128)S(1)} %collective-permute-done.refs_1_), channel_id=1, source_target_pairs={{0,1},{1,0},{2,3},{3,2},{4,5},{5,4},{6,7},{7,6},{8,9},{9,8},{10,11... | collective-permute-start | bytes 73736 | tf_op jit(solution)/shard_map/ppermute | solution.py:195
  7.2 0.0 collective-permute-done.3.both_ref.refs_4_
  7.2 0.4 %collective-permute-start.4 = (f32[48,128]{1,0:T(8,128)S(1)}, f32[48,128]{1,0:T(8,128)S(1)}, u32[]{:S(2)}, u32[]{:S(2)}) collective-permute-start(f32[48,128]{1,0:T(8,128)S(1)} %first_half.1), channel_id=1, source_target_pairs={{0,1},{1,0},{2,3},{3,2},{4,5},{5,4},{6,7},{7,6},{8,9},{9,8},{10,11... | collective-permute-start | bytes 73736 | tf_op jit(solution)/shard_map/ppermute | solution.py:195
  7.6 0.7 %prepare.1.refs_0_ = s32[3,8,128]{2,1,0:T(8,128)S(1)} custom-call(s32[2,8]{1,0:T(2,128)} %refs_0_.1), custom_call_target="tpu_custom_call" | custom-call | tf_op jit(solution)/shard_map/prepare/pallas_call | solution.py:225
  8.3 0.0 collective-permute-done.1.refs_2_
  8.3 0.3 %collective-permute-done.5.refs_6_ = f32[48,128]{1,0:T(8,128)S(1)} collective-permute-done((f32[48,128]{1,0:T(8,128)S(1)}, f32[48,128]{1,0:T(8,128)S(1)}, u32[]{:S(2)}, u32[]{:S(2)}) %collective-permute-start.5) | collective-permute-done | bytes 24608 | tf_op jit(solution)/shard_map/ppermute | solution.py:195
  8.6 0.0 collective-permute-done.4.refs_5_
  8.6 1.2 %tiles.1 = f32[2,2,2]{2,1,0:T(2,128)} custom-call(s32[3,8,128]{2,1,0:T(8,128)S(1)} %prepare.1.refs_0_, f32[48,128]{1,0:T(8,128)S(1)} %collective-permute-done.refs_1_, f32[48,128]{1,0:T(8,128)S(1)} %collective-permute-done.1.refs_2_, f32[96,128]{1,0:T(8,128)S(1)} %join.1.refs_3_, f32[96,128]{1,0:T(8,128)S(1)} %collective-permute-done.3.both_ref.refs_4_, ...), custom_call_target="tpu_custom_call" | custom-call | tf_op jit(solution)/shard_map/tiles/pallas_call | solution.py:232
  (5 shorter events, 0.0 us)
Async XLA Ops:
  0.0 3.1 %collective-permute-start.2 = (f32[48,128]{1,0:T(8,128)}, f32[48,128]{1,0:T(8,128)S(1)}, u32[]{:S(2)}, u32[]{:S(2)}) collective-permute-start(f32[48,128]{1,0:T(8,128)} %bitcast.5), channel_id=1, source_target_pairs={{0,1},{1,0},{2,3},{3,2},{4,5},{5,4},{6,7},{7,6},{8,9},{9,8},{10,11... | collective-permute-start | bytes 73736 | tf_op jit(solution)/shard_map/ppermute | solution.py:195
  0.5 2.7 %copy-start = (f32[2,3,1024]{2,0,1:T(2,128)S(1)}, f32[2,3,1024]{2,0,1:T(2,128)}, u32[]{:S(2)}) copy-start(f32[2,3,1024]{2,0,1:T(2,128)} %param.2) | copy-start | bytes 73732
  0.5 6.6 %collective-permute-start = (f32[48,128]{1,0:T(8,128)}, f32[48,128]{1,0:T(8,128)S(1)}, u32[]{:S(2)}, u32[]{:S(2)}) collective-permute-start(f32[48,128]{1,0:T(8,128)} %bitcast.6), channel_id=1, source_target_pairs={{0,3},{1,2},{2,5},{3,4},{4,7},{5,6},{6,1},{7,0},{8,11},{9,10},{10,... | collective-permute-start | bytes 73736 | tf_op jit(solution)/shard_map/ppermute | solution.py:195
  3.2 4.0 %collective-permute-start.3 = (f32[96,128]{1,0:T(8,128)S(1)}, f32[96,128]{1,0:T(8,128)S(1)}, u32[]{:S(2)}, u32[]{:S(2)}) collective-permute-start(f32[96,128]{1,0:T(8,128)S(1)} %join.1.refs_3_), channel_id=1, source_target_pairs={{0,17},{1,8},{2,19},{3,10},{4,21},{5,12},{6,23},{7,14},{8,25},{9,0... | collective-permute-start | bytes 147464 | tf_op jit(solution)/shard_map/ppermute | solution.py:195
  4.4 4.2 %collective-permute-start.5 = (f32[48,128]{1,0:T(8,128)S(1)}, f32[48,128]{1,0:T(8,128)S(1)}, u32[]{:S(2)}, u32[]{:S(2)}) collective-permute-start(f32[48,128]{1,0:T(8,128)S(1)} %relay.3), channel_id=1, source_target_pairs={{0,25},{1,24},{2,27},{3,26},{4,29},{5,28},{6,31},{7,30},{8,17},{9,... | collective-permute-start | bytes 73736 | tf_op jit(solution)/shard_map/ppermute | solution.py:195
  7.0 1.2 %collective-permute-start.1 = (f32[48,128]{1,0:T(8,128)S(1)}, f32[48,128]{1,0:T(8,128)S(1)}, u32[]{:S(2)}, u32[]{:S(2)}) collective-permute-start(f32[48,128]{1,0:T(8,128)S(1)} %collective-permute-done.refs_1_), channel_id=1, source_target_pairs={{0,1},{1,0},{2,3},{3,2},{4,5},{5,4},{6,7},{7,6},{8,9},{9,8},{10,11... | collective-permute-start | bytes 73736 | tf_op jit(solution)/shard_map/ppermute | solution.py:195
  7.2 1.4 %collective-permute-start.4 = (f32[48,128]{1,0:T(8,128)S(1)}, f32[48,128]{1,0:T(8,128)S(1)}, u32[]{:S(2)}, u32[]{:S(2)}) collective-permute-start(f32[48,128]{1,0:T(8,128)S(1)} %first_half.1), channel_id=1, source_target_pairs={{0,1},{1,0},{2,3},{3,2},{4,5},{5,4},{6,7},{7,6},{8,9},{9,8},{10,11... | collective-permute-start | bytes 73736 | tf_op jit(solution)/shard_map/ppermute | solution.py:195

commit v8 on v7

--- a/solution.py
+++ b/solution.py
@@ -46,8 +46,12 @@
     near_out[...] = near_ref[...]
 
 
-def first_half(both_ref, half_out):
-    half_out[...] = both_ref[pl.ds(0, half_out.shape[0])]
+def handed(far_ref, *refs):
+    pair_refs, out = refs[:-1], refs[-1]
+    rows = far_ref.shape[0]
+    out[pl.ds(0, rows)] = far_ref[...]
+    for n, ref in enumerate(pair_refs, 1):
+        out[pl.ds(n * rows, rows)] = ref[pl.ds(0, rows)]
 
 
 def prepare(row_source, slots, roots_ref, pick_out):
@@ -129,12 +133,16 @@
         return jnp.where(flags[None], first, second).reshape(-1, LANES)
 
     odd = pick_ref[n_tiles] == 1
-    cols = [channels(chosen(odd, both_ref[pl.ds(3 * rows, 3 * rows)], far_ref[...])), channels(passed_ref[...])]
+    cols = [channels(chosen(odd, both_ref[pl.ds(3 * rows, 3 * rows)], far_ref[...])), channels(passed_ref[pl.ds(0, 3 * rows)])]
+    row_blocks = []
+    for n in range(passed_ref.shape[0] // (3 * rows) - 1):
+        row_blocks += [(row_refs[n], 3 * rows), (passed_ref, (n + 1) * 3 * rows)]
+    row_blocks += [(ref, 0) for ref in row_refs[len(row_blocks) // 2:]]
     row_values = []
     for s in range(n_tiles):
         value = both_ref[pl.ds(0, 3 * rows)]
-        for n, ref in enumerate(row_refs, 1):
-            value = chosen(pick_ref[s] == n, ref[pl.ds(ref.shape[0] - 3 * rows, 3 * rows)], value)
+        for n, (ref, at) in enumerate(row_blocks, 1):
+            value = chosen(pick_ref[s] == n, ref[pl.ds(at, 3 * rows)], value)
         row_values.append(channels(value))
 
     def dot(first, second):
@@ -212,30 +220,32 @@
     ahead, tile = lax.optimization_barrier((packed, tile))
     far = moved(ahead, lambda i, j: (i, ((j + 2) % n_col) ^ 1))
     both = on_core(join, double, packed, on_core(relay, single, near, flops=3000000), tile)
-    row_blocks, slots = [], []
+    pairs_in, slots = [], []
     for k in range(1, n_row - 1, 2):
-        pair = moved(both, lambda i, j, k=k: (row_target(i, k + 1 if j % 2 == 0 else k), j ^ 1))
-        swapped = moved(on_core(first_half, single, pair), lambda i, j: (i, j ^ 1))
-        row_blocks += [pair, swapped]
+        pairs_in.append(moved(both, lambda i, j, k=k: (row_target(i, k + 1 if j % 2 == 0 else k), j ^ 1)))
         slots += [(k, k + 1), (k + 1, k)]
+    lone = []
     if n_row % 2 == 0:
-        row_blocks.append(moved(on_core(relay, single, near, flops=20_000_000_000), lambda i, j: (row_target(i, n_row - 1), j ^ 1)))
+        payload = on_core(relay, single, near, flops=20_000_000_000)
+        lone.append(moved(payload, lambda i, j: (row_target(i, n_row - 1), j ^ 1)))
         slots.append((n_row - 1, n_row - 1))
-    passed = moved(far, lambda i, j: (i, j ^ 1))
+    stack = pltpu.VMEM(((1 + len(pairs_in)) * packed.shape[0], LANES), jnp.float32)
+    passed = moved(on_core(handed, stack, far, *pairs_in), lambda i, j: (i, j ^ 1))
     pick = pl.pallas_call(
         lambda *refs: prepare(row_source, slots, *refs),
         out_shape=pltpu.VMEM((n_tiles + 1, 8, LANES), jnp.int32),
         in_specs=[pl.BlockSpec(memory_space=pltpu.SMEM)],
         out_specs=vmem,
+        cost_estimate=pl.CostEstimate(flops=20_000_000_000, bytes_accessed=0, transcendentals=0),
         name="prepare",
     )(roots)
     return pl.pallas_call(
         lambda *refs: kernel(n_tiles, *refs),
         out_shape=jax.ShapeDtypeStruct((n_tiles, block, block), jnp.float32),
-        in_specs=[vmem] * (4 + len(row_blocks)),
+        in_specs=[vmem] * (4 + len(pairs_in) + len(lone)),
         out_specs=vmem,
         name="tiles",
-    )(*map(placed, [pick, far, passed, both, *row_blocks]))
+    )(*map(placed, [pick, far, passed, both, *pairs_in, *lone]))
 
 
 def solution(mesh):

time: 9.97 us -> 9.96 us (level)
  waiting for transfers between devices: 1.4 us -> 1.74 us
  starting transfers between devices: 6.4 us -> 6.07 us
    ppermute x6 -> x5, waiting for transfers between devices: 1.4 us -> 1.74 us  [moved(): return lax.ppermute(value, ('row', 'col'), pairs)]
    ppermute x6 -> x5, starting transfers between devices: 6.4 us -> 6.07 us  [moved(): return lax.ppermute(value, ('row', 'col'), pairs)]
  transfers between devices with their start and end apart: 6 -> 5, of which waited for: 2 -> 2; matrix products, arithmetic and copies ran while one was open for 0% -> 0% of each run, Pallas kernels for 7% -> 7%
where the time goes in v8:
time: 9.96 us; the launch traced here: 9.8 us
  starting transfers between devices  6.07 us (61%)
  Pallas kernels  1.96 us (20%)
  waiting for transfers between devices  1.74 us (17%)
    ppermute x5, starting transfers between devices, moved(): return lax.ppermute(value, ('row', 'col'), pairs)  6.07 us
    ppermute x5, waiting for transfers between devices, moved(): return lax.ppermute(value, ('row', 'col'), pairs)  1.74 us
    pallas_call x1, Pallas kernels, local(): pl.pallas_call(lambda *refs: kernel(n_tiles, *refs), out_shape=jax.ShapeD...  1.24 us
    pallas_call x1, Pallas kernels, local(): pl.pallas_call(lambda *refs: prepare(row_source, slots, *refs), out_shape...  0.71 us
  transfers between devices with their start and end apart: 5, of which 2 were waited for; matrix products, arithmetic and copies ran while one was open for 0% of the time, Pallas kernels for 7%

profile of v8, /device:TPU:0, one launch (start us, length us, event | category | flops | bytes accessed | tf_op | source)
XLA Modules:
  0.0 9.8 jit_solution(5197449133840225192)
XLA Ops:
  0.0 0.5 %collective-permute-start.1 = (f32[48,128]{1,0:T(8,128)}, f32[48,128]{1,0:T(8,128)S(1)}, u32[]{:S(2)}, u32[]{:S(2)}) collective-permute-start(f32[48,128]{1,0:T(8,128)} %bitcast.5), channel_id=1, source_target_pairs={{0,1},{1,0},{2,3},{3,2},{4,5},{5,4},{6,7},{7,6},{8,9},{9,8},{10,11... | collective-permute-start | bytes 73736 | tf_op jit(solution)/shard_map/ppermute | solution.py:203
  0.5 0.0 copy-start
  0.5 2.7 %collective-permute-start = (f32[48,128]{1,0:T(8,128)}, f32[48,128]{1,0:T(8,128)S(1)}, u32[]{:S(2)}, u32[]{:S(2)}) collective-permute-start(f32[48,128]{1,0:T(8,128)} %bitcast.6), channel_id=1, source_target_pairs={{0,3},{1,2},{2,5},{3,4},{4,7},{5,6},{6,1},{7,0},{8,11},{9,10},{10,... | collective-permute-start | bytes 73736 | tf_op jit(solution)/shard_map/ppermute | solution.py:203
  3.1 0.0 collective-permute-done.1.near_ref
  3.2 0.0 copy-done
  3.2 1.2 %collective-permute-start.2 = (f32[96,128]{1,0:T(8,128)S(1)}, f32[96,128]{1,0:T(8,128)S(1)}, u32[]{:S(2)}, u32[]{:S(2)}) collective-permute-start(f32[96,128]{1,0:T(8,128)S(1)} %join.1.refs_3_), channel_id=1, source_target_pairs={{0,17},{1,8},{2,19},{3,10},{4,21},{5,12},{6,23},{7,14},{8,25},{9,0... | collective-permute-start | bytes 147464 | tf_op jit(solution)/shard_map/ppermute | solution.py:203
  4.4 1.5 %collective-permute-start.4 = (f32[48,128]{1,0:T(8,128)S(1)}, f32[48,128]{1,0:T(8,128)S(1)}, u32[]{:S(2)}, u32[]{:S(2)}) collective-permute-start(f32[48,128]{1,0:T(8,128)S(1)} %relay.3), channel_id=1, source_target_pairs={{0,25},{1,24},{2,27},{3,26},{4,29},{5,28},{6,31},{7,30},{8,17},{9,... | collective-permute-start | bytes 73736 | tf_op jit(solution)/shard_map/ppermute | solution.py:203
  5.9 1.1 %collective-permute-done.far_ref.refs_1_ = f32[48,128]{1,0:T(8,128)S(1)} collective-permute-done((f32[48,128]{1,0:T(8,128)}, f32[48,128]{1,0:T(8,128)S(1)}, u32[]{:S(2)}, u32[]{:S(2)}) %collective-permute-start) | collective-permute-done | bytes 24608 | tf_op jit(solution)/shard_map/ppermute | solution.py:203
  7.0 0.0 collective-permute-done.2.refs_0_.refs_4_
  7.0 0.2 %collective-permute-start.3 = (f32[96,128]{1,0:T(8,128)S(1)}, f32[96,128]{1,0:T(8,128)S(1)}, u32[]{:S(2)}, u32[]{:S(2)}) collective-permute-start(f32[96,128]{1,0:T(8,128)S(1)} %handed.1), channel_id=1, source_target_pairs={{0,1},{1,0},{2,3},{3,2},{4,5},{5,4},{6,7},{7,6},{8,9},{9,8},{10,11... | collective-permute-start | bytes 147464 | tf_op jit(solution)/shard_map/ppermute | solution.py:203
  7.2 0.7 %prepare.1.refs_0_ = s32[3,8,128]{2,1,0:T(8,128)S(1)} custom-call(s32[2,8]{1,0:T(2,128)} %refs_0_.1), custom_call_target="tpu_custom_call" | custom-call | flops 20000000000 | tf_op jit(solution)/shard_map/prepare/pallas_call | solution.py:234
  7.9 0.6 %collective-permute-done.4.refs_5_ = f32[48,128]{1,0:T(8,128)S(1)} collective-permute-done((f32[48,128]{1,0:T(8,128)S(1)}, f32[48,128]{1,0:T(8,128)S(1)}, u32[]{:S(2)}, u32[]{:S(2)}) %collective-permute-start.4) | collective-permute-done | bytes 24608 | tf_op jit(solution)/shard_map/ppermute | solution.py:203
  8.6 0.0 collective-permute-done.3.refs_2_
  8.6 1.2 %tiles.1 = f32[2,2,2]{2,1,0:T(2,128)} custom-call(s32[3,8,128]{2,1,0:T(8,128)S(1)} %prepare.1.refs_0_, f32[48,128]{1,0:T(8,128)S(1)} %collective-permute-done.far_ref.refs_1_, f32[96,128]{1,0:T(8,128)S(1)} %collective-permute-done.3.refs_2_, f32[96,128]{1,0:T(8,128)S(1)} %join.1.refs_3_, f32[96,128]{1,0:T(8,128)S(1)} %collective-permute-done.2.refs_0_.refs_4_, ...), custom_call_target="tpu_custom_call" | custom-call | tf_op jit(solution)/shard_map/tiles/pallas_call | solution.py:242
  (5 shorter events, 0.0 us)
Async XLA Ops:
  0.0 3.1 %collective-permute-start.1 = (f32[48,128]{1,0:T(8,128)}, f32[48,128]{1,0:T(8,128)S(1)}, u32[]{:S(2)}, u32[]{:S(2)}) collective-permute-start(f32[48,128]{1,0:T(8,128)} %bitcast.5), channel_id=1, source_target_pairs={{0,1},{1,0},{2,3},{3,2},{4,5},{5,4},{6,7},{7,6},{8,9},{9,8},{10,11... | collective-permute-start | bytes 73736 | tf_op jit(solution)/shard_map/ppermute | solution.py:203
  0.5 2.7 %copy-start = (f32[2,3,1024]{2,0,1:T(2,128)S(1)}, f32[2,3,1024]{2,0,1:T(2,128)}, u32[]{:S(2)}) copy-start(f32[2,3,1024]{2,0,1:T(2,128)} %param.2) | copy-start | bytes 73732
  0.5 6.6 %collective-permute-start = (f32[48,128]{1,0:T(8,128)}, f32[48,128]{1,0:T(8,128)S(1)}, u32[]{:S(2)}, u32[]{:S(2)}) collective-permute-start(f32[48,128]{1,0:T(8,128)} %bitcast.6), channel_id=1, source_target_pairs={{0,3},{1,2},{2,5},{3,4},{4,7},{5,6},{6,1},{7,0},{8,11},{9,10},{10,... | collective-permute-start | bytes 73736 | tf_op jit(solution)/shard_map/ppermute | solution.py:203
  3.2 3.9 %collective-permute-start.2 = (f32[96,128]{1,0:T(8,128)S(1)}, f32[96,128]{1,0:T(8,128)S(1)}, u32[]{:S(2)}, u32[]{:S(2)}) collective-permute-start(f32[96,128]{1,0:T(8,128)S(1)} %join.1.refs_3_), channel_id=1, source_target_pairs={{0,17},{1,8},{2,19},{3,10},{4,21},{5,12},{6,23},{7,14},{8,25},{9,0... | collective-permute-start | bytes 147464 | tf_op jit(solution)/shard_map/ppermute | solution.py:203
  4.4 4.2 %collective-permute-start.4 = (f32[48,128]{1,0:T(8,128)S(1)}, f32[48,128]{1,0:T(8,128)S(1)}, u32[]{:S(2)}, u32[]{:S(2)}) collective-permute-start(f32[48,128]{1,0:T(8,128)S(1)} %relay.3), channel_id=1, source_target_pairs={{0,25},{1,24},{2,27},{3,26},{4,29},{5,28},{6,31},{7,30},{8,17},{9,... | collective-permute-start | bytes 73736 | tf_op jit(solution)/shard_map/ppermute | solution.py:203
  7.0 1.5 %collective-permute-start.3 = (f32[96,128]{1,0:T(8,128)S(1)}, f32[96,128]{1,0:T(8,128)S(1)}, u32[]{:S(2)}, u32[]{:S(2)}) collective-permute-start(f32[96,128]{1,0:T(8,128)S(1)} %handed.1), channel_id=1, source_target_pairs={{0,1},{1,0},{2,3},{3,2},{4,5},{5,4},{6,7},{7,6},{8,9},{9,8},{10,11... | collective-permute-start | bytes 147464 | tf_op jit(solution)/shard_map/ppermute | solution.py:203

commit v9 on v8

--- a/solution.py
+++ b/solution.py
@@ -221,14 +221,14 @@
     far = moved(ahead, lambda i, j: (i, ((j + 2) % n_col) ^ 1))
     both = on_core(join, double, packed, on_core(relay, single, near, flops=3000000), tile)
     pairs_in, slots = [], []
-    for k in range(1, n_row - 1, 2):
+    for k in range(2, n_row, 2):
         pairs_in.append(moved(both, lambda i, j, k=k: (row_target(i, k + 1 if j % 2 == 0 else k), j ^ 1)))
         slots += [(k, k + 1), (k + 1, k)]
     lone = []
     if n_row % 2 == 0:
         payload = on_core(relay, single, near, flops=20_000_000_000)
-        lone.append(moved(payload, lambda i, j: (row_target(i, n_row - 1), j ^ 1)))
-        slots.append((n_row - 1, n_row - 1))
+        lone.append(moved(payload, lambda i, j: (row_target(i, 1), j ^ 1)))
+        slots.append((1, 1))
     stack = pltpu.VMEM(((1 + len(pairs_in)) * packed.shape[0], LANES), jnp.float32)
     passed = moved(on_core(handed, stack, far, *pairs_in), lambda i, j: (i, j ^ 1))
     pick = pl.pallas_call(

time: 9.96 us -> 9.99 us (level)
  starting transfers between devices: 6.07 us -> 6.45 us
  waiting for transfers between devices: 1.74 us -> 1.39 us
    ppermute x5, starting transfers between devices: 6.07 us -> 6.45 us  [moved(): return lax.ppermute(value, ('row', 'col'), pairs)]
    ppermute x5, waiting for transfers between devices: 1.74 us -> 1.39 us  [moved(): return lax.ppermute(value, ('row', 'col'), pairs)]
  transfers between devices with their start and end apart: 5 -> 5, of which waited for: 2 -> 3; matrix products, arithmetic and copies ran while one was open for 0% -> 0% of each run, Pallas kernels for 7% -> 7%
where the time goes in v9:
time: 9.99 us; the launch traced here: 9.83 us
  starting transfers between devices  6.45 us (65%)
  Pallas kernels  1.96 us (20%)
  waiting for transfers between devices  1.39 us (14%)
    ppermute x5, starting transfers between devices, moved(): return lax.ppermute(value, ('row', 'col'), pairs)  6.45 us
    ppermute x5, waiting for transfers between devices, moved(): return lax.ppermute(value, ('row', 'col'), pairs)  1.39 us
    pallas_call x1, Pallas kernels, local(): pl.pallas_call(lambda *refs: kernel(n_tiles, *refs), out_shape=jax.ShapeD...  1.24 us
    pallas_call x1, Pallas kernels, local(): pl.pallas_call(lambda *refs: prepare(row_source, slots, *refs), out_shape...  0.71 us
  transfers between devices with their start and end apart: 5, of which 3 were waited for; matrix products, arithmetic and copies ran while one was open for 0% of the time, Pallas kernels for 7%

profile of v9, /device:TPU:0, one launch (start us, length us, event | category | flops | bytes accessed | tf_op | source)
XLA Modules:
  0.0 9.8 jit_solution(14850295918512767333)
XLA Ops:
  0.0 0.5 %collective-permute-start.1 = (f32[48,128]{1,0:T(8,128)}, f32[48,128]{1,0:T(8,128)S(1)}, u32[]{:S(2)}, u32[]{:S(2)}) collective-permute-start(f32[48,128]{1,0:T(8,128)} %bitcast.5), channel_id=1, source_target_pairs={{0,1},{1,0},{2,3},{3,2},{4,5},{5,4},{6,7},{7,6},{8,9},{9,8},{10,11... | collective-permute-start | bytes 73736 | tf_op jit(solution)/shard_map/ppermute | solution.py:203
  0.5 0.0 copy-start
  0.5 2.7 %collective-permute-start = (f32[48,128]{1,0:T(8,128)}, f32[48,128]{1,0:T(8,128)S(1)}, u32[]{:S(2)}, u32[]{:S(2)}) collective-permute-start(f32[48,128]{1,0:T(8,128)} %bitcast.6), channel_id=1, source_target_pairs={{0,3},{1,2},{2,5},{3,4},{4,7},{5,6},{6,1},{7,0},{8,11},{9,10},{10,... | collective-permute-start | bytes 73736 | tf_op jit(solution)/shard_map/ppermute | solution.py:203
  3.1 0.0 collective-permute-done.1.near_ref
  3.2 0.0 copy-done
  3.2 2.2 %collective-permute-start.2 = (f32[96,128]{1,0:T(8,128)S(1)}, f32[96,128]{1,0:T(8,128)S(1)}, u32[]{:S(2)}, u32[]{:S(2)}) collective-permute-start(f32[96,128]{1,0:T(8,128)S(1)} %join.1.refs_3_), channel_id=1, source_target_pairs={{0,25},{1,16},{2,27},{3,18},{4,29},{5,20},{6,31},{7,22},{8,17},{9,... | collective-permute-start | bytes 147464 | tf_op jit(solution)/shard_map/ppermute | solution.py:203
  5.3 0.6 %collective-permute-start.4 = (f32[48,128]{1,0:T(8,128)S(1)}, f32[48,128]{1,0:T(8,128)S(1)}, u32[]{:S(2)}, u32[]{:S(2)}) collective-permute-start(f32[48,128]{1,0:T(8,128)S(1)} %relay.3), channel_id=1, source_target_pairs={{0,9},{1,8},{2,11},{3,10},{4,13},{5,12},{6,15},{7,14},{8,1},{9,0},... | collective-permute-start | bytes 73736 | tf_op jit(solution)/shard_map/ppermute | solution.py:203
  6.0 1.1 %collective-permute-done.far_ref.refs_1_ = f32[48,128]{1,0:T(8,128)S(1)} collective-permute-done((f32[48,128]{1,0:T(8,128)}, f32[48,128]{1,0:T(8,128)S(1)}, u32[]{:S(2)}, u32[]{:S(2)}) %collective-permute-start) | collective-permute-done | bytes 24608 | tf_op jit(solution)/shard_map/ppermute | solution.py:203
  7.0 0.1 %collective-permute-done.2.refs_0_.refs_4_ = f32[96,128]{1,0:T(8,128)S(1)} collective-permute-done((f32[96,128]{1,0:T(8,128)S(1)}, f32[96,128]{1,0:T(8,128)S(1)}, u32[]{:S(2)}, u32[]{:S(2)}) %collective-permute-start.2) | collective-permute-done | bytes 49184 | tf_op jit(solution)/shard_map/ppermute | solution.py:203
  7.2 0.5 %collective-permute-start.3 = (f32[96,128]{1,0:T(8,128)S(1)}, f32[96,128]{1,0:T(8,128)S(1)}, u32[]{:S(2)}, u32[]{:S(2)}) collective-permute-start(f32[96,128]{1,0:T(8,128)S(1)} %handed.1), channel_id=1, source_target_pairs={{0,1},{1,0},{2,3},{3,2},{4,5},{5,4},{6,7},{7,6},{8,9},{9,8},{10,11... | collective-permute-start | bytes 147464 | tf_op jit(solution)/shard_map/ppermute | solution.py:203
  7.7 0.7 %prepare.1.refs_0_ = s32[3,8,128]{2,1,0:T(8,128)S(1)} custom-call(s32[2,8]{1,0:T(2,128)} %refs_0_.1), custom_call_target="tpu_custom_call" | custom-call | flops 20000000000 | tf_op jit(solution)/shard_map/prepare/pallas_call | solution.py:234
  8.4 0.2 %collective-permute-done.4.refs_5_ = f32[48,128]{1,0:T(8,128)S(1)} collective-permute-done((f32[48,128]{1,0:T(8,128)S(1)}, f32[48,128]{1,0:T(8,128)S(1)}, u32[]{:S(2)}, u32[]{:S(2)}) %collective-permute-start.4) | collective-permute-done | bytes 24608 | tf_op jit(solution)/shard_map/ppermute | solution.py:203
  8.6 0.0 collective-permute-done.3.refs_2_
  8.6 1.2 %tiles.1 = f32[2,2,2]{2,1,0:T(2,128)} custom-call(s32[3,8,128]{2,1,0:T(8,128)S(1)} %prepare.1.refs_0_, f32[48,128]{1,0:T(8,128)S(1)} %collective-permute-done.far_ref.refs_1_, f32[96,128]{1,0:T(8,128)S(1)} %collective-permute-done.3.refs_2_, f32[96,128]{1,0:T(8,128)S(1)} %join.1.refs_3_, f32[96,128]{1,0:T(8,128)S(1)} %collective-permute-done.2.refs_0_.refs_4_, ...), custom_call_target="tpu_custom_call" | custom-call | tf_op jit(solution)/shard_map/tiles/pallas_call | solution.py:242
  (5 shorter events, 0.0 us)
Async XLA Ops:
  0.0 3.1 %collective-permute-start.1 = (f32[48,128]{1,0:T(8,128)}, f32[48,128]{1,0:T(8,128)S(1)}, u32[]{:S(2)}, u32[]{:S(2)}) collective-permute-start(f32[48,128]{1,0:T(8,128)} %bitcast.5), channel_id=1, source_target_pairs={{0,1},{1,0},{2,3},{3,2},{4,5},{5,4},{6,7},{7,6},{8,9},{9,8},{10,11... | collective-permute-start | bytes 73736 | tf_op jit(solution)/shard_map/ppermute | solution.py:203
  0.5 2.7 %copy-start = (f32[2,3,1024]{2,0,1:T(2,128)S(1)}, f32[2,3,1024]{2,0,1:T(2,128)}, u32[]{:S(2)}) copy-start(f32[2,3,1024]{2,0,1:T(2,128)} %param.2) | copy-start | bytes 73732
  0.5 6.6 %collective-permute-start = (f32[48,128]{1,0:T(8,128)}, f32[48,128]{1,0:T(8,128)S(1)}, u32[]{:S(2)}, u32[]{:S(2)}) collective-permute-start(f32[48,128]{1,0:T(8,128)} %bitcast.6), channel_id=1, source_target_pairs={{0,3},{1,2},{2,5},{3,4},{4,7},{5,6},{6,1},{7,0},{8,11},{9,10},{10,... | collective-permute-start | bytes 73736 | tf_op jit(solution)/shard_map/ppermute | solution.py:203
  3.2 4.0 %collective-permute-start.2 = (f32[96,128]{1,0:T(8,128)S(1)}, f32[96,128]{1,0:T(8,128)S(1)}, u32[]{:S(2)}, u32[]{:S(2)}) collective-permute-start(f32[96,128]{1,0:T(8,128)S(1)} %join.1.refs_3_), channel_id=1, source_target_pairs={{0,25},{1,16},{2,27},{3,18},{4,29},{5,20},{6,31},{7,22},{8,17},{9,... | collective-permute-start | bytes 147464 | tf_op jit(solution)/shard_map/ppermute | solution.py:203
  5.3 3.3 %collective-permute-start.4 = (f32[48,128]{1,0:T(8,128)S(1)}, f32[48,128]{1,0:T(8,128)S(1)}, u32[]{:S(2)}, u32[]{:S(2)}) collective-permute-start(f32[48,128]{1,0:T(8,128)S(1)} %relay.3), channel_id=1, source_target_pairs={{0,9},{1,8},{2,11},{3,10},{4,13},{5,12},{6,15},{7,14},{8,1},{9,0},... | collective-permute-start | bytes 73736 | tf_op jit(solution)/shard_map/ppermute | solution.py:203
  7.2 1.4 %collective-permute-start.3 = (f32[96,128]{1,0:T(8,128)S(1)}, f32[96,128]{1,0:T(8,128)S(1)}, u32[]{:S(2)}, u32[]{:S(2)}) collective-permute-start(f32[96,128]{1,0:T(8,128)S(1)} %handed.1), channel_id=1, source_target_pairs={{0,1},{1,0},{2,3},{3,2},{4,5},{5,4},{6,7},{7,6},{8,9},{9,8},{10,11... | collective-permute-start | bytes 147464 | tf_op jit(solution)/shard_map/ppermute | solution.py:203
